TPU v7x, 128 devices: a whole 4x4x4 slice. The times are simulated.
128 devices in a mesh: step: 8 (over y, x_lo), head: 8 (over z, core), fsdp: 2 (over x_hi).
Axes of the slice: x: 4 (x_hi: 2, x_lo: 2; x = x_hi * 2 + x_lo), y: 4, z: 4, core: 2. Of those that a mesh axis runs over, the one named last changes fastest.
Arguments:
- states: float32 [8, 2, 1024, 5120], P('step', 'fsdp', 'head'), may hold values from -10.5 to 10.5
- timesteps: int32 [8, 2], P('step'), may hold values from 0 to 1000, as said below
- lengths: int32 [2], P('fsdp'), may hold values from 512 to 1024, as said below
- modulation: float32 [8, 3, 5120], P('step'), may hold values from -4 to 4
- w_query: bfloat16 [5120, 3072], P(('step', 'fsdp'), 'head'), may hold values from -0.1118034 to 0.1118034
- w_key: bfloat16 [5120, 3072], P(('step', 'fsdp'), 'head'), may hold values from -0.1118034 to 0.1118034
- w_value: bfloat16 [5120, 3072], P(('step', 'fsdp'), 'head'), may hold values from -0.078125 to 0.078125
- w_out: bfloat16 [3072, 5120], P('head', ('step', 'fsdp')), may hold values from -0.109375 to 0.109375
- q_gain: float32 [3072], P('head'), may hold values from 0.5 to 12
- k_gain: float32 [3072], P('head'), may hold values from 0.5 to 12
Outputs:
- next_states: float32 [8, 2, 1024, 5120], P('step', 'fsdp', 'head')
- update: bfloat16 [8, 2, 1024, 5120], P('step', 'fsdp', 'head')
Inputs may be any that keep to these rules, and one draw needn't show every extreme that they name: `timesteps`: A row holds a step's start above its end; each row's end is the next row's start; the first row starts at 1000 and the last ends at 0. `lengths`: positions from a clip's length on are padding; at least one clip is full.
All inputs are finite; a program needn't handle non-finite values.
Results may differ from a plain program's by a relative error of at most 0.02.
The roundings to bfloat16 on the way count: a program that leaves them out, or rounds other values in their place, can miss the bound.
Values may be sent and summed in bfloat16 or wider, within the bound.
A program may use at most 128 MiB of HBM per device.

v0:
```python
import math

import jax
import jax.numpy as jnp
from jax import lax
from jax.sharding import PartitionSpec as P

HD = 128


def prefix(x, axis, combine, identity):
    peers, position = (lax.axis_size(axis), lax.axis_index(axis))
    everything = lax.all_gather(x.astype(jnp.bfloat16), axis)
    start = jnp.broadcast_to(jnp.asarray(identity, x.dtype), x.shape)

    def lap(k, before):
        reached = k < position
        new = combine(before, everything[k].astype(x.dtype))
        return jnp.where(reached, new, before)

    return lax.fori_loop(0, peers, lap, start)


def normed_rows(current, shift_row, scale_row):
    centre = jnp.mean(current, axis=-1, keepdims=True)
    centred = current - centre
    spread = jnp.mean(centred * centred, axis=-1, keepdims=True)
    return (centred * lax.rsqrt(spread + 1e-06) * (1.0 + scale_row) + shift_row).astype(
        jnp.bfloat16
    )


def scaled_heads(values, square_sum, full_width, gain_vec):
    row_count = values.shape[0]
    square = (square_sum / full_width)[:, None]
    normed = (values * lax.rsqrt(square + 1e-06) * gain_vec).astype(jnp.bfloat16)
    return normed.reshape(row_count, values.shape[1] // HD, HD)


def add_terms(earlier, following):
    return earlier + following


def body(states, timesteps, lengths, modulation, w_query, w_key, w_value, w_out, q_gain, k_gain):
    current = states[0, 0]
    modulated = normed_rows(current, modulation[0, 0], modulation[0, 1])
    gathered = lax.all_gather(modulated, "head", axis=0, tiled=True)
    total_tokens = gathered.shape[0]
    local_inner = w_query.shape[1]
    pieces = (
        lax.all_gather(w_query, ("step", "fsdp"), axis=0, tiled=True),
        lax.all_gather(w_key, ("step", "fsdp"), axis=0, tiled=True),
        lax.all_gather(w_value, ("step", "fsdp"), axis=0, tiled=True),
    )
    query_raw, key_raw, value_raw = tuple(
        (jnp.dot(gathered, piece_rows, preferred_element_type=jnp.float32) for piece_rows in pieces)
    )
    full_width = float(local_inner * lax.axis_size("head"))
    query_square, key_square = lax.psum(
        (jnp.sum(query_raw * query_raw, axis=1), jnp.sum(key_raw * key_raw, axis=1)), "head"
    )
    queries = scaled_heads(query_raw, query_square, full_width, q_gain)
    keys_normed = scaled_heads(key_raw, key_square, full_width, k_gain)
    value_rows = value_raw.astype(jnp.bfloat16).reshape(total_tokens, -1, HD)
    scores = jnp.einsum(
        "qhd,khd->hqk", queries, keys_normed, preferred_element_type=jnp.float32
    ) * (1.0 / math.sqrt(HD))
    valid_keys = lax.iota(jnp.int32, total_tokens) < lengths[0]
    scores = jnp.where(valid_keys[None, None, :], scores, -jnp.inf)
    highest = jnp.max(scores, axis=-1, keepdims=True)
    raised = jnp.exp(scores - highest)
    soft_rows = (raised / jnp.sum(raised, axis=-1, keepdims=True)).astype(jnp.bfloat16)
    attended = jnp.einsum("hqk,khd->qhd", soft_rows, value_rows, preferred_element_type=jnp.float32)
    attended = attended.astype(jnp.bfloat16).reshape(total_tokens, local_inner)
    out_full = lax.all_gather(w_out, ("step", "fsdp"), axis=1, tiled=True)
    projected = lax.psum_scatter(
        jnp.dot(attended, out_full, preferred_element_type=jnp.float32).astype(jnp.bfloat16),
        "head",
        scatter_dimension=0,
        tiled=True,
    ).astype(jnp.float32)
    gate_row = modulation[0, 2]
    branch = gate_row * projected
    update = branch.astype(jnp.bfloat16)
    step_width = (timesteps[0, 1] - timesteps[0, 0]).astype(jnp.float32) / 1000.0
    drift_term = step_width * (current + branch)
    anchor = jnp.where(lax.axis_index("step") == 0, current, jnp.zeros_like(current))
    carried = drift_term + anchor
    before = prefix(carried, "step", add_terms, jnp.zeros_like(carried))
    reached = before + carried
    return (reached[None, None], update[None, None])


def solution(mesh):
    in_specs = (
        P("step", "fsdp", "head", None),
        P("step", None),
        P("fsdp"),
        P("step", None, None),
        P(("step", "fsdp"), "head"),
        P(("step", "fsdp"), "head"),
        P(("step", "fsdp"), "head"),
        P("head", ("step", "fsdp")),
        P("head"),
        P("head"),
    )
    out_specs = (P("step", "fsdp", "head", None), P("step", "fsdp", "head", None))
    return jax.shard_map(body, mesh=mesh, in_specs=in_specs, out_specs=out_specs, check_vma=False)
```

profile of v0, /device:TPU:24, one launch (start us, length us, event | category | flops | bytes accessed | tf_op | source)
XLA Modules:
  0.0 782.5 jit_solution(11154526217884984067)
XLA Ops:
  14.6 92.5 %all-gather.12.cloned.1.call-done = bf16[5120,384]{1,0:T(8,128)(2,1)} async-done(((bf16[320,384]{1,0:T(8,128)(2,1)}), bf16[5120,384]{1,0:T(8,128)(2,1)}) %all-gather.12.cloned.1.call-update) | async-done | bytes 3932176 | tf_op jit(solution)/shard_map/all_gather | solution.py:51
  107.1 62.6 %all-gather.8.cloned.1.call-done = bf16[1024,5120]{1,0:T(8,128)(2,1)} async-done(((bf16[128,5120]{1,0:T(8,128)(2,1)}), bf16[1024,5120]{1,0:T(8,128)(2,1)}) %all-gather.8.cloned.1.call-update) | async-done | bytes 10485776 | tf_op jit(solution)/shard_map/all_gather | solution.py:47
  169.6 10.5 %multiply_reduce_fusion.2 = (f32[1024]{0:T(1024)S(1)}, f32[1024,384]{0,1:T(8,128)}) fusion(bf16[1024,5120]{1,0:T(8,128)(2,1)} %all-gather.8.cloned.1.call-done, bf16[5120,384]{1,0:T(8,128)(2,1)} %all-gather.12.cloned.1.call-done), kind=kOutput, calls=%fused_computation.24 | convolution fusion | flops 4027317248 | bytes 15994880 | tf_op jit(solution)/shard_map/dot_general | solution.py:56
  180.1 86.6 %all-gather.14.cloned.1.call-done = bf16[5120,384]{1,0:T(8,128)(2,1)} async-done(((bf16[320,384]{1,0:T(8,128)(2,1)}), bf16[5120,384]{1,0:T(8,128)(2,1)}) %all-gather.14.cloned.1.call-update) | async-done | bytes 3932176 | tf_op jit(solution)/shard_map/all_gather | solution.py:52
  266.7 10.5 %multiply_reduce_fusion.1 = (f32[1024]{0:T(1024)S(1)}, f32[1024,384]{0,1:T(8,128)}) fusion(bf16[1024,5120]{1,0:T(8,128)(2,1)} %all-gather.8.cloned.1.call-done, bf16[5120,384]{1,0:T(8,128)(2,1)} %all-gather.14.cloned.1.call-done), kind=kOutput, calls=%fused_computation.22 | convolution fusion | flops 4027317248 | bytes 15994880 | tf_op jit(solution)/shard_map/dot_general | solution.py:56
  277.3 13.2 %all-reduce = (f32[1024]{0:T(1024)S(1)}, f32[1024]{0:T(1024)S(1)}) all-reduce(f32[1024]{0:T(1024)S(1)} %get-tuple-element.114, f32[1024]{0:T(1024)S(1)} %get-tuple-element.116), channel_id=1, replica_groups=mesh['step'=8,'head'=8,'fsdp'=2] {'head'}, use_global_device_ids=true, to_apply=%region_3.0 | all-reduce | flops 2048 | bytes 16384 | tf_op jit(solution)/shard_map/psum | solution.py:59
  293.5 10.1 %fusion.18 = (f32[3,1024]{1,0:T(4,128)S(1)}, f32[3,1024,1024]{1,2,0:T(8,128)}) fusion(pred[1024]{0:T(1024)(128)(4,1)S(1)} %iota_compare_fusion, bf16[1024,3,128]{0,2,1:T(8,128)(2,1)S(1)} %bitcast.54, bf16[1024,3,128]{0,2,1:T(8,128)(2,1)} %bitcast.55), kind=kOutput, calls=%fused_computation.40 | convolution fusion | flops 817890304 | bytes 14169088 | tf_op jit(solution)/shard_map/sub | solution.py:71
  303.5 61.5 %all-gather.10.cloned.1.call-done = bf16[5120,384]{1,0:T(8,128)(2,1)} async-done(((bf16[320,384]{1,0:T(8,128)(2,1)}), bf16[5120,384]{1,0:T(8,128)(2,1)}) %all-gather.10.cloned.1.call-update) | async-done | bytes 3932176 | tf_op jit(solution)/shard_map/all_gather | solution.py:53
  365.1 9.3 %convolution_convert_fusion.1 = bf16[1024,384]{0,1:T(8,128)(2,1)S(1)} fusion(bf16[1024,5120]{1,0:T(8,128)(2,1)} %all-gather.8.cloned.1.call-done, bf16[5120,384]{1,0:T(8,128)(2,1)} %all-gather.10.cloned.1.call-done), kind=kOutput, calls=%fused_computation.25 | convolution fusion | flops 4026925056 | bytes 15204352 | tf_op jit(solution)/shard_map/dot_general | solution.py:56
  374.4 5.7 fusion.9
  380.2 84.1 %all-gather.16.cloned.1.call-done = bf16[384,5120]{0,1:T(8,128)(2,1)} async-done(((bf16[384,320]{0,1:T(8,128)(2,1)}), bf16[384,5120]{0,1:T(8,128)(2,1)}) %all-gather.16.cloned.1.call-update) | async-done | bytes 3932176 | tf_op jit(solution)/shard_map/all_gather | solution.py:75
  464.2 10.4 %convolution_convert_fusion = bf16[1024,5120]{1,0:T(8,128)(2,1)} fusion(bf16[1024,384]{0,1:T(8,128)(2,1)S(1)} %bitcast.60, bf16[384,5120]{0,1:T(8,128)(2,1)} %all-gather.16.cloned.1.call-done), kind=kOutput, calls=%fused_computation.6 | convolution fusion | flops 4031774720 | bytes 15204352 | tf_op jit(solution)/shard_map/dot_general | solution.py:77
  477.1 61.3 %reduce-scatter.2.cloned.1.call-done = bf16[128,5120]{1,0:T(8,128)(2,1)} async-done(((bf16[1024,5120]{1,0:T(8,128)(2,1)}), bf16[128,5120]{1,0:T(8,128)(2,1)}) %reduce-scatter.2.cloned.1.call-update) | async-done | bytes 1310736 | tf_op jit(solution)/shard_map/reduce_scatter | solution.py:76
  538.4 2.9 fusion.13
  541.4 207.3 %all-gather.18.cloned.1.call-done = bf16[1024,5120]{1,0:T(8,128)(2,1)} async-done(((bf16[128,5120]{1,0:T(8,128)(2,1)}), bf16[1024,5120]{1,0:T(8,128)(2,1)}) %all-gather.18.cloned.1.call-update) | async-done | bytes 10485776 | tf_op jit(solution)/shard_map/all_gather | solution.py:13
  748.6 22.3 %while.14 = (s32[]{:T(128)}, f32[128,5120]{1,0:T(8,128)S(1)}, s32[]{:T(128)}, bf16[8,128,5120]{2,1,0:T(8,128)(2,1)}, s32[]{:T(128)}, /*index=5*/s32[]{:T(128)}) while((s32[]{:T(128)}, f32[128,5120]{1,0:T(8,128)S(1)}, s32[]{:T(128)}, bf16[8,128,5120]{2,1,0:T(8,128)(2,1)}, s32[]{:T(128)}, /*index=5*/s32[]{:T(128)}) %tuple.61), condition=%wide.region_10.11_spmd.clone, body=%wide.region_9.10_spmd.clone.sunk | while | flops 2621444 | bytes 6553701 | solution.py:21
  751.4 2.8 add_select_fusion.2
  754.2 2.8 add_select_fusion.2
  757.0 2.8 add_select_fusion.2
  759.8 2.8 add_select_fusion.2
  762.6 2.8 add_select_fusion.2
  765.4 2.8 add_select_fusion.2
  768.2 2.8 add_select_fusion.2
  770.9 4.8 fusion.12
  (39 shorter events, 13.6 us)
Async XLA Ops:
  7.2 2.8 copy-start
  7.2 99.9 %all-gather.12.cloned.1.call-start = ((), (), s32[]{:S(2)}) async-start(), calls=%async_computation.3 | async-start | bytes 4177920 | tf_op jit(solution)/shard_map/all_gather | solution.py:51
  7.9 2.5 copy-start.2
  7.9 161.7 %all-gather.8.cloned.1.call-start = ((), (), s32[]{:S(2)}) async-start(), calls=%async_computation.1 | async-start | bytes 11796480 | tf_op jit(solution)/shard_map/all_gather | solution.py:47
  12.0 254.7 %all-gather.14.cloned.1.call-start = ((), (), s32[]{:S(2)}) async-start(), calls=%async_computation.4 | async-start | bytes 4177920 | tf_op jit(solution)/shard_map/all_gather | solution.py:52
  12.7 352.3 %all-gather.10.cloned.1.call-start = ((), (), s32[]{:S(2)}) async-start(), calls=%async_computation.2 | async-start | bytes 4177920 | tf_op jit(solution)/shard_map/all_gather | solution.py:53
  13.3 450.9 %all-gather.16.cloned.1.call-start = ((), (), s32[]{:S(2)}) async-start(), calls=%async_computation.5 | async-start | bytes 4177920 | tf_op jit(solution)/shard_map/all_gather | solution.py:75
  13.9 524.5 %reduce-scatter.2.cloned.1.call-start = ((), (), s32[]{:S(2)}) async-start(), calls=%async_computation.6 | async-start | bytes 11796480 | tf_op jit(solution)/shard_map/reduce_scatter | solution.py:76
  180.1 110.4 %copy-start.4 = (f32[384]{0:T(512)S(1)}, f32[384]{0:T(512)}, u32[]{:S(2)}) copy-start(f32[384]{0:T(512)} %param.20) | copy-start | bytes 4612
  180.1 112.1 %copy-start.5 = (f32[384]{0:T(512)S(1)}, f32[384]{0:T(512)}, u32[]{:S(2)}) copy-start(f32[384]{0:T(512)} %param.21) | copy-start | bytes 4612
  290.5 1.9 copy-start.1
  474.6 0.7 copy-start.3
  474.6 274.0 %all-gather.18.cloned.1.call-start = ((), (), s32[]{:S(2)}) async-start(), calls=%async_computation.7 | async-start | bytes 11796480 | tf_op jit(solution)/shard_map/all_gather | solution.py:13
Sparse Core Ops, SparseCore 0:
  9.7 97.3 all-gather.11
  109.3 60.2 all-gather.7
  171.3 95.3 all-gather.13
  268.2 96.7 all-gather.9
  366.5 97.6 all-gather.15
  474.7 63.6 reduce-scatter.1
  541.5 207.1 all-gather.17
where the time goes:
time: 784 us; the launch traced here: 783 us
  waiting for transfers between devices  658 us (84%)
  matrix products  56.5 us (7%)
  other arithmetic  36.6 us (5%)
  between operations  16.2 us (2%)
  blocking collectives  13.2 us (2%)
    all_gather x1, waiting for transfers between devices, prefix(): everything = lax.all_gather(x.astype(jnp.bfloat16), axis)  207 us
    all_gather x1, waiting for transfers between devices, body(): lax.all_gather(w_query, ('step', 'fsdp'), axis=0, tiled=True)  92.5 us
    all_gather x1, waiting for transfers between devices, body(): lax.all_gather(w_key, ('step', 'fsdp'), axis=0, tiled=True)  86.6 us
    all_gather x1, waiting for transfers between devices, body(): out_full = lax.all_gather(w_out, ('step', 'fsdp'), axis=1, tiled=True)  84.1 us
    all_gather x1, waiting for transfers between devices, body(): gathered = lax.all_gather(modulated, 'head', axis=0, tiled=True)  62.6 us
    all_gather x1, waiting for transfers between devices, body(): lax.all_gather(w_value, ('step', 'fsdp'), axis=0, tiled=True)  61.5 us
    reduce_scatter x1, waiting for transfers between devices, body(): lax.psum_scatter(jnp.dot(attended, out_full, preferred_element_type=jnp.f...  61.3 us
    dot_general x3, matrix products, body(): jnp.dot(gathered, piece_rows, preferred_element_type=jnp.float32)  30.4 us
  transfers between devices with their start and end apart: 7, of which 7 were waited for; matrix products, arithmetic and copies ran while one was open for 7% of the time, Pallas kernels for 0%

commit v1 on v0

v1 whole, which is shorter than its diff:
```python
import math

import jax
import jax.numpy as jnp
from jax import lax
from jax.experimental import pallas as pl
from jax.experimental.pallas import tpu as pltpu
from jax.sharding import PartitionSpec as P

HD = 128
BF16 = jnp.bfloat16
F32 = jnp.float32
MESH = pl.DeviceIdType.MESH
NJ = 8
CW = 640
TOK = 128
LOCAL = 384
DEPTH = 320
HALF = 160
QUART = 80


class Link:
    def __init__(self, send, recv):
        self.send, self.recv, self.used = send, recv, 0

    def take(self, n=1):
        first = self.used
        self.used += n
        return first

    def copy(self, src, dst, sem, to):
        return pltpu.make_async_remote_copy(
            src_ref=src,
            dst_ref=dst,
            send_sem=self.send.at[sem],
            recv_sem=self.recv.at[sem],
            device_id=to,
            device_id_type=MESH,
        )


class Place:
    def __init__(self):
        step, head, fsdp = (lax.axis_index(a) for a in ("step", "head", "fsdp"))
        self.step, self.head = step, head
        self.y, self.x_lo, self.x_hi = step // 2, step % 2, fsdp
        self.x = self.x_hi * 2 + self.x_lo
        self.z, self.core = head // 2, head % 2

    def at(self, dx=0, dy=0, dz=0, other_core=False):
        x, y, z = (self.x + dx) % 4, (self.y + dy) % 4, (self.z + dz) % 4
        core = 1 - self.core if other_core else self.core
        return (y * 2 + x % 2, z * 2 + core, x // 2)

    def column(self, dx):
        x = (self.x + dx) % 4
        return (x % 2) * 2 + x // 2

    def row(self, dy):
        return (self.y + dy) % 4


class PlaneGather:
    def __init__(self, link, place, own, full):
        self.link, self.me, self.own, self.full = link, place, own, full
        self.base = link.take(16)
        self.started = []

    def go(self, slot, src, dst, to):
        copy = self.link.copy(src, dst, self.base + slot, to)
        copy.start()
        self.started.append(copy)

    def got(self, slot, dst):
        self.link.copy(dst, dst, self.base + slot, self.me.at(dx=1)).wait_recv()

    def start1(self):
        me, g = self.me, self.full
        y, c = me.y, me.column(0)
        g[y, c, 0] = self.own[0:HALF, :]
        g[y, c, 1] = self.own[HALF:DEPTH, :]
        a, b = self.own.at[0:HALF], self.own.at[HALF:DEPTH]
        self.go(0, a, g.at[y, c, 0], me.at(dx=1))
        self.go(1, a, g.at[y, c, 0], me.at(dx=-1))
        self.go(2, b, g.at[y, c, 1], me.at(dy=1))
        self.go(3, b, g.at[y, c, 1], me.at(dy=-1))

    def start2(self):
        me, g = self.me, self.full
        y, c = me.y, me.column(0)
        left, right = me.column(-1), me.column(1)
        below, above = me.row(-1), me.row(1)
        self.got(0, g.at[y, left, 0])
        part = g.at[y, left, 0, 0:QUART]
        self.go(4, part, part, me.at(dx=1))
        self.got(1, g.at[y, right, 0])
        part = g.at[y, right, 0, QUART:HALF]
        self.go(5, part, part, me.at(dx=-1))
        self.got(2, g.at[below, c, 1])
        part = g.at[below, c, 1, 0:QUART]
        self.go(6, part, part, me.at(dy=1))
        self.got(3, g.at[above, c, 1])
        part = g.at[above, c, 1, QUART:HALF]
        self.go(7, part, part, me.at(dy=-1))

    def start3(self):
        me, g = self.me, self.full
        y, c = me.y, me.column(0)
        far_x, far_y = me.column(2), me.row(2)
        self.got(4, g.at[y, far_x, 0, 0:QUART])
        self.got(5, g.at[y, far_x, 0, QUART:HALF])
        part = g.at[y, :, 0]
        self.go(8, part, part, me.at(dy=1))
        self.go(9, part, part, me.at(dy=-1))
        self.got(6, g.at[far_y, c, 1, 0:QUART])
        self.got(7, g.at[far_y, c, 1, QUART:HALF])
        part = g.at[:, c, 1]
        self.go(10, part, part, me.at(dx=1))
        self.go(11, part, part, me.at(dx=-1))

    def start4(self):
        me, g = self.me, self.full
        left, right = me.column(-1), me.column(1)
        below, above = me.row(-1), me.row(1)
        self.got(8, g.at[below, :, 0])
        part = g.at[below, :, 0, 0:QUART]
        self.go(12, part, part, me.at(dy=1))
        self.got(9, g.at[above, :, 0])
        part = g.at[above, :, 0, QUART:HALF]
        self.go(13, part, part, me.at(dy=-1))
        self.got(10, g.at[:, left, 1])
        part = g.at[:, left, 1, 0:QUART]
        self.go(14, part, part, me.at(dx=1))
        self.got(11, g.at[:, right, 1])
        part = g.at[:, right, 1, QUART:HALF]
        self.go(15, part, part, me.at(dx=-1))

    def finish(self):
        me, g = self.me, self.full
        far_x, far_y = me.column(2), me.row(2)
        self.got(12, g.at[far_y, :, 0, 0:QUART])
        self.got(13, g.at[far_y, :, 0, QUART:HALF])
        self.got(14, g.at[:, far_x, 1, 0:QUART])
        self.got(15, g.at[:, far_x, 1, QUART:HALF])
        for copy in self.started:
            copy.wait_send()


class TokenGather:
    def __init__(self, link, place, acts):
        self.link, self.me, self.acts = link, place, acts
        self.base = link.take(9)
        self.started = []

    def rows(self, dz, other=False, start=0, size=TOK):
        me = self.me
        z = (me.z + dz) % 4
        core = 1 - me.core if other else me.core
        return self.acts.at[pl.ds(pl.multiple_of((z * 2 + core) * TOK + start, 64), size), :]

    def go(self, slot, part, to):
        copy = self.link.copy(part, part, self.base + slot, to)
        copy.start()
        self.started.append(copy)

    def got(self, slot, part):
        self.link.copy(part, part, self.base + slot, self.me.at(dz=1)).wait_recv()

    def start1(self):
        me = self.me
        own = self.rows(0)
        self.go(0, own, me.at(dz=1))
        self.go(1, own, me.at(dz=-1))
        self.go(2, own, me.at(other_core=True))

    def start2(self):
        me = self.me
        self.got(0, self.rows(-1))
        self.go(3, self.rows(-1, size=64), me.at(dz=1))
        self.got(1, self.rows(1))
        self.go(4, self.rows(1, start=64, size=64), me.at(dz=-1))
        self.go(5, self.rows(-1), me.at(other_core=True))
        self.go(6, self.rows(1), me.at(other_core=True))

    def start3(self):
        me = self.me
        self.got(3, self.rows(2, size=64))
        self.go(7, self.rows(2, size=64), me.at(other_core=True))
        self.got(4, self.rows(2, start=64, size=64))
        self.go(8, self.rows(2, start=64, size=64), me.at(other_core=True))

    def finish(self):
        self.got(2, self.rows(0, other=True))
        self.got(5, self.rows(-1, other=True))
        self.got(6, self.rows(1, other=True))
        self.got(7, self.rows(2, other=True, size=64))
        self.got(8, self.rows(2, other=True, start=64, size=64))
        for copy in self.started:
            copy.wait_send()


def eye_mask():
    return lax.broadcasted_iota(jnp.int32, (128, 128), 0) == lax.broadcasted_iota(
        jnp.int32, (128, 128), 1
    )


def kernel(
    length_ref,
    width_ref,
    states_ref,
    mod_ref,
    gain_ref,
    wqk_ref,
    wv_ref,
    wo_ref,
    next_ref,
    update_ref,
    acts,
    qk_full,
    v_full,
    o_full,
    raw,
    qk,
    value,
    attended,
    squares,
    partial,
    summed,
    z_first,
    z_second,
    pair_out,
    pair_in,
    chain_out,
    chain_in,
    back_out,
    back_in,
    send_sem,
    recv_sem,
):
    me = Place()
    link = Link(send_sem, recv_sem)

    barrier = pltpu.get_barrier_semaphore()
    for d in range(1, 8):
        pl.semaphore_signal(
            barrier,
            inc=1,
            device_id=(me.step, (me.head + d) % 8, me.x_hi),
            device_id_type=MESH,
        )
    for to in (me.at(dx=1), me.at(dx=-1), me.at(dy=1), me.at(dy=-1)):
        pl.semaphore_signal(barrier, inc=1, device_id=to, device_id_type=MESH)
    pl.semaphore_wait(barrier, 11)

    w_qk = PlaneGather(link, me, wqk_ref, qk_full)
    w_v = PlaneGather(link, me, wv_ref, v_full)
    w_o = PlaneGather(link, me, wo_ref, o_full)
    tokens = TokenGather(link, me, acts)

    with jax.named_scope("norm"):
        w_qk.start1()
        shift, scale = mod_ref[0:1, :], 1.0 + mod_ref[1:2, :]

        @pl.loop(0, 8)
        def _(r):
            x = states_ref[pl.ds(r * 16, 16), :]
            centred = x - jnp.mean(x, axis=-1, keepdims=True)
            spread = jnp.mean(centred * centred, axis=-1, keepdims=True)
            y = centred * lax.rsqrt(spread + 1e-06) * scale + shift
            acts[pl.ds(pl.multiple_of(me.head * TOK + r * 16, 16), 16), :] = y.astype(BF16)

        tokens.start1()
    with jax.named_scope("qk_second"):
        w_qk.start2()
    with jax.named_scope("qk_third"):
        w_qk.start3()
        w_v.start1()
    with jax.named_scope("tokens_second"):
        tokens.start2()
    with jax.named_scope("qk_fourth"):
        w_qk.start4()
        w_v.start2()
    with jax.named_scope("tokens_third"):
        tokens.start3()
    with jax.named_scope("qk_finish"):
        w_qk.finish()
        w_v.start3()
        w_o.start1()
    with jax.named_scope("tokens_finish"):
        tokens.finish()

    with jax.named_scope("qk_matmul"):

        @pl.loop(0, 4)
        def _(m):
            rows = pl.ds(pl.multiple_of(m * 256, 256), 256)
            product = jnp.dot(
                acts[rows, :],
                qk_full[...].reshape(5120, 2 * LOCAL),
                preferred_element_type=F32,
            )
            raw[rows, :] = product
            for part in range(2):
                for b in range(2):
                    p = product[b * 128 : b * 128 + 128, part * LOCAL : (part + 1) * LOCAL]
                    total = jnp.sum(p * p, axis=1, keepdims=True)
                    row = jnp.sum(jnp.where(eye_mask(), total, 0.0), axis=0, keepdims=True)
                    squares[me.head, pl.ds(part * 8 + m * 2 + b, 1), :] = row

    with jax.named_scope("squares"):
        base = link.take(7)
        sent = []
        for d in range(1, 8):
            mine = squares.at[me.head]
            copy = link.copy(mine, mine, base + d - 1, (me.step, (me.head + d) % 8, me.x_hi))
            copy.start()
            sent.append(copy)
        w_v.start4()
        w_o.start2()
        for d in range(1, 8):
            theirs = squares.at[(me.head - d) % 8]
            link.copy(theirs, theirs, base + d - 1, (me.step, (me.head + d) % 8, me.x_hi)).wait_recv()
        for copy in sent:
            copy.wait_send()

    with jax.named_scope("qk_norm"):

        @pl.loop(0, 8)
        def _(b):
            rows = pl.ds(pl.multiple_of(b * 128, 128), 128)
            for part in range(2):
                total = squares[0, pl.ds(part * 8 + b, 1), :]
                for d in range(1, 8):
                    total = total + squares[d, pl.ds(part * 8 + b, 1), :]
                factor = lax.rsqrt(total / 3072.0 + 1e-06)
                column = jnp.sum(jnp.where(eye_mask(), factor, 0.0), axis=1, keepdims=True)
                cols = slice(part * LOCAL, (part + 1) * LOCAL)
                qk[rows, cols] = (raw[rows, cols] * column * gain_ref[part : part + 1, :]).astype(BF16)

    with jax.named_scope("v_finish"):
        w_v.finish()
        w_o.start3()

    with jax.named_scope("v_matmul"):

        @pl.loop(0, 4)
        def _(m):
            rows = pl.ds(pl.multiple_of(m * 256, 256), 256)
            product = jnp.dot(
                acts[rows, :], v_full[...].reshape(5120, LOCAL), preferred_element_type=F32
            )
            value[rows, :] = product.astype(BF16)

    with jax.named_scope("o_fourth"):
        w_o.start4()

    with jax.named_scope("attention"):
        length = length_ref[0]

        @pl.loop(0, 4)
        def _(m):
            rows = pl.ds(pl.multiple_of(m * 256, 256), 256)
            valid = lax.broadcasted_iota(jnp.int32, (256, 1024), 1) < length
            for h in range(3):
                q = qk[rows, h * HD : (h + 1) * HD]
                k = qk[:, LOCAL + h * HD : LOCAL + (h + 1) * HD]
                s = lax.dot_general(q, k, (((1,), (1,)), ((), ())), preferred_element_type=F32)
                s = jnp.where(valid, s * (1.0 / math.sqrt(HD)), -jnp.inf)
                e = jnp.exp(s - jnp.max(s, axis=-1, keepdims=True))
                p = (e * (1.0 / jnp.sum(e, axis=-1, keepdims=True))).astype(BF16)
                o = jnp.dot(p, value[:, h * HD : (h + 1) * HD], preferred_element_type=F32)
                attended[rows, h * HD : (h + 1) * HD] = o.astype(BF16)

    with jax.named_scope("o_finish"):
        w_o.finish()

    sib, first, second = link.take(NJ), link.take(2 * NJ), link.take(2 * NJ)
    pair, chain, back = link.take(NJ), link.take(NJ), link.take(NJ)
    up, down = me.at(dz=1), me.at(dz=-1)
    above, below, far = (me.z + 1) % 4, (me.z - 1) % 4, (me.z + 2) % 4
    partner = (me.y * 2 + 1 - me.x_lo, me.head, me.x_hi)
    y_up = me.at(dy=1)
    mine = pl.ds(pl.multiple_of(me.x_lo * 64, 64), 64)
    other = pl.ds(pl.multiple_of((1 - me.x_lo) * 64, 64), 64)
    width = width_ref[0]
    on_low = me.x_lo == 0

    def sib_copy(j):
        return link.copy(
            partial.at[j % 2, :, 1 - me.core], summed.at[j], sib + j, me.at(other_core=True)
        )

    def first_copies(j):
        return (
            link.copy(summed.at[j, far, 0:64], z_first.at[j, 0], first + 2 * j, up),
            link.copy(summed.at[j, far, 64:128], z_first.at[j, 1], first + 2 * j + 1, down),
        )

    def second_copies(j):
        return (
            link.copy(summed.at[j, above], z_second.at[j, 0], second + 2 * j, up),
            link.copy(summed.at[j, below], z_second.at[j, 1], second + 2 * j + 1, down),
        )

    def pair_copy(j):
        return link.copy(pair_out.at[j], pair_in.at[j], pair + j, partner)

    def chain_copy(j):
        return link.copy(chain_out.at[j], chain_in.at[j], chain + j, y_up)

    def back_copy(j):
        return link.copy(back_out.at[j], back_in.at[j], back + j, partner)

    def project(j):
        w = o_full[j // 2, pl.ds((j % 2) * 2, 2)].reshape(CW, LOCAL)
        for m in range(4):
            p = lax.dot_general(
                attended[m * 256 : (m + 1) * 256, :],
                w,
                (((1,), (1,)), ((), ())),
                preferred_element_type=F32,
            ).astype(BF16)
            partial[j % 2, m, 0] = p[0:128]
            partial[j % 2, m, 1] = p[128:256]
        sib_copy(j).start()

    def add_sibling(j):
        copy = sib_copy(j)
        copy.wait_recv()
        for m in range(4):
            own = partial[j % 2, m, me.core].astype(F32)
            summed[j, m] = (own + summed[j, m].astype(F32)).astype(BF16)
        copy.wait_send()
        for c in first_copies(j):
            c.start()

    def add_far(j):
        copies = first_copies(j)
        for c in copies:
            c.wait_recv()
        summed[j, above, 0:64] = (
            summed[j, above, 0:64].astype(F32) + z_first[j, 0].astype(F32)
        ).astype(BF16)
        summed[j, below, 64:128] = (
            summed[j, below, 64:128].astype(F32) + z_first[j, 1].astype(F32)
        ).astype(BF16)
        for c in second_copies(j):
            c.start()
        for c in copies:
            c.wait_send()

    def drift(j):
        copies = second_copies(j)
        for c in copies:
            c.wait_recv()
        cols = pl.ds(pl.multiple_of(j * CW, 128), CW)
        projected = (
            summed[j, me.z].astype(F32) + z_second[j, 0].astype(F32) + z_second[j, 1].astype(F32)
        )
        branch = mod_ref[2:3, cols] * projected
        update_ref[:, cols] = branch.astype(BF16)
        current = states_ref[:, cols]
        anchor = jnp.where(me.step == 0, current, 0.0)
        next_ref[:, cols] = width * (current + branch) + anchor
        pair_out[j] = next_ref[other, cols].astype(BF16)
        pair_copy(j).start()
        for c in copies:
            c.wait_send()

    def run_chain(j):
        cols = pl.ds(pl.multiple_of(j * CW, 128), CW)
        p_copy, c_copy = pair_copy(j), chain_copy(j)
        p_copy.wait_recv()
        received = pair_in[j].astype(F32)
        own = next_ref[mine, cols]

        @pl.when(me.y > 0)
        def _():
            c_copy.wait_recv()

        @pl.when(me.y == 0)
        def _():
            chain_in[j] = jnp.zeros((64, CW), BF16)

        earlier = chain_in[j].astype(F32)

        @pl.when(me.y < 3)
        def _():
            chain_out[j] = (earlier + own + received).astype(BF16)
            c_copy.start()

        back_out[j] = (earlier + jnp.where(on_low, own, 0.0)).astype(BF16)
        back_copy(j).start()
        next_ref[mine, cols] = own + (earlier + jnp.where(on_low, 0.0, received))
        p_copy.wait_send()

    def add_back(j):
        cols = pl.ds(pl.multiple_of(j * CW, 128), CW)
        copy = back_copy(j)
        copy.wait_recv()
        next_ref[other, cols] = next_ref[other, cols] + back_in[j].astype(F32)
        copy.wait_send()

        @pl.when(me.y < 3)
        def _():
            chain_copy(j).wait_send()

    with jax.named_scope("reduce"):
        stages = (project, add_sibling, add_far, drift, run_chain, add_back)

        @pl.loop(0, NJ + len(stages) - 1)
        def _(i):
            for lag, stage in enumerate(stages):
                j = i - lag

                @pl.when((j >= 0) & (j < NJ))
                def _(stage=stage, j=j):
                    stage(j)


def body(states, timesteps, lengths, modulation, w_query, w_key, w_value, w_out, q_gain, k_gain):
    width = (timesteps[0, 1] - timesteps[0, 0]).astype(F32) / 1000.0
    n_sems = 3 * 16 + 9 + 7 + 8 * NJ
    vmem = pl.BlockSpec(memory_space=pltpu.VMEM)
    smem = pl.BlockSpec(memory_space=pltpu.SMEM)
    nxt, update = pl.pallas_call(
        kernel,
        out_shape=(
            jax.ShapeDtypeStruct((TOK, 5120), F32),
            jax.ShapeDtypeStruct((TOK, 5120), BF16),
        ),
        in_specs=[smem, smem] + [vmem] * 6,
        out_specs=(vmem, vmem),
        scratch_shapes=[
            pltpu.VMEM((1024, 5120), BF16),
            pltpu.VMEM((4, 4, 2, HALF, 2 * LOCAL), BF16),
            pltpu.VMEM((4, 4, 2, HALF, LOCAL), BF16),
            pltpu.VMEM((4, 4, 2, HALF, LOCAL), BF16),
            pltpu.VMEM((1024, 2 * LOCAL), F32),
            pltpu.VMEM((1024, 2 * LOCAL), BF16),
            pltpu.VMEM((1024, LOCAL), BF16),
            pltpu.VMEM((1024, LOCAL), BF16),
            pltpu.VMEM((8, 16, 128), F32),
            pltpu.VMEM((2, 4, 2, TOK, CW), BF16),
            pltpu.VMEM((NJ, 4, TOK, CW), BF16),
            pltpu.VMEM((NJ, 2, 64, CW), BF16),
            pltpu.VMEM((NJ, 2, TOK, CW), BF16),
            pltpu.VMEM((NJ, 64, CW), BF16),
            pltpu.VMEM((NJ, 64, CW), BF16),
            pltpu.VMEM((NJ, 64, CW), BF16),
            pltpu.VMEM((NJ, 64, CW), BF16),
            pltpu.VMEM((NJ, 64, CW), BF16),
            pltpu.VMEM((NJ, 64, CW), BF16),
            pltpu.SemaphoreType.DMA((n_sems,)),
            pltpu.SemaphoreType.DMA((n_sems,)),
        ],
        compiler_params=pltpu.CompilerParams(
            collective_id=0,
            has_side_effects=True,
            vmem_limit_bytes=63 * 1024 * 1024,
        ),
    )(
        lengths,
        width.reshape(1),
        states[0, 0],
        modulation[0],
        jnp.stack([q_gain, k_gain]),
        jnp.concatenate([w_query, w_key], axis=1),
        w_value,
        w_out.T,
    )
    return (nxt[None, None], update[None, None])


def solution(mesh):
    in_specs = (
        P("step", "fsdp", "head", None),
        P("step", None),
        P("fsdp"),
        P("step", None, None),
        P(("step", "fsdp"), "head"),
        P(("step", "fsdp"), "head"),
        P(("step", "fsdp"), "head"),
        P("head", ("step", "fsdp")),
        P("head"),
        P("head"),
    )
    out_specs = (P("step", "fsdp", "head", None), P("step", "fsdp", "head", None))
    return jax.shard_map(body, mesh=mesh, in_specs=in_specs, out_specs=out_specs, check_vma=False)
```

time: 784 us -> 183 us (0.23)
  waiting for transfers between devices: 658 us -> 0 us
  Pallas kernels: 0 us -> 169 us
  matrix products: 56.5 us -> 0 us
  other arithmetic: 36.6 us -> 2.47 us
  between operations: 16.2 us -> 2.6 us
  blocking collectives: 13.2 us -> 0 us
    all_gather x6 -> x0, waiting for transfers between devices: 595 us -> none  [the longest x1 207 us: prefix(): everything = lax.all_gather(x.astype(jnp.bfloat16), axis)]
    pallas_call x0 -> x1, Pallas kernels: none -> 169 us  [body(): pl.pallas_call(kernel, out_shape=(jax.ShapeDtypeStruct((TOK, 5120), F32),...]
    reduce_scatter x1 -> x0, waiting for transfers between devices: 61.3 us -> none  [body(): lax.psum_scatter(jnp.dot(attended, out_full, preferred_element_type=jnp.f...]
    dot_general x5 -> x0, matrix products: 46.5 us -> none  [the longest x3 30.4 us: body(): jnp.dot(gathered, piece_rows, preferred_element_type=jnp.float32)]
    select_n x8 -> x0, other arithmetic: 22.1 us -> none  [lap(): return jnp.where(reached, new, before)]
    psum x1 -> x0, blocking collectives: 13.2 us -> none  [body(): lax.psum((jnp.sum(query_raw * query_raw, axis=1), jnp.sum(key_raw * key_r...]
    sub x1 -> x0, matrix products: 10.1 us -> none  [body(): raised = jnp.exp(scores - highest)]
  transfers between devices with their start and end apart: 7 -> 0, of which waited for: 7 -> 0; matrix products, arithmetic and copies ran while one was open for 7% -> 0% of each run, Pallas kernels for 0% -> 0%
where the time goes in v1:
time: 183 us
  Pallas kernels  169 us (92%)
  local copies, waits for them, and re-layouts  8.81 us (5%)
  between operations  2.6 us (1%)
  other arithmetic  2.47 us (1%)
    pallas_call x1, Pallas kernels, body(): pl.pallas_call(kernel, out_shape=(jax.ShapeDtypeStruct((TOK, 5120), F32),...  169 us
    unnamed x5, local copies, waits for them, and re-layouts  6.13 us

profile of v1, /device:TPU:24, one launch (start us, length us, event | category | flops | bytes accessed | tf_op | source)
XLA Modules:
  0.0 182.7 jit_solution(10150051326094818929)
XLA Ops:
  1.3 1.3 fusion
  3.9 0.7 stack.9
  4.6 0.7 stack.10
  5.3 0.6 pad_maximum_fusion.1.gain_ref
  5.9 1.5 copy.14
  7.3 1.9 %pad_maximum_fusion.wqk_ref = bf16[320,768]{1,0:T(8,128)(2,1)} fusion(bf16[320,384]{1,0:T(8,128)(2,1)} %param.15, bf16[320,384]{1,0:T(8,128)(2,1)} %param.14), kind=kLoop, calls=%fused_computation | loop fusion | flops 983040 | bytes 983040 | tf_op jit(solution)/shard_map/concatenate | solution.py:570
  9.2 168.8 %shard_map.113 = (f32[128,5120]{1,0:T(8,128)}, bf16[128,5120]{1,0:T(8,128)(2,1)}) custom-call(s32[1]{0:T(128)S(6)} %copy.17.length_ref, f32[1]{0:T(128)} %bitcast.width_ref, f32[128,5120]{1,0:T(8,128)} %bitcast.8, f32[3,5120]{1,0:T(4,128)} %bitcast.11, f32[2,384]{1,0:T(2,128)} %pad_maximum_fusion.1.gain_ref, bf16[320,768]{1,0:T(8,128)(2,1)} %pad_maximum_fusion.wqk_ref, ...), custom_call_target="tpu_custom_call" | custom-call | tf_op jit(solution)/shard_map/pallas_call | solution.py:528
  178.1 0.0 copy-start
  178.1 3.6 %copy.18 = f32[1,1,128,5120]{3,2,1,0:T(8,128)} copy(f32[1,1,128,5120]{3,2,1,0:T(8,128)} %bitcast.9) | data formatting | bytes 5242880
  181.7 0.0 copy-done
  181.7 1.1 copy.19
Async XLA Ops:
  178.1 3.6 %copy-start = (bf16[128,5120]{1,0:T(8,128)(2,1)S(1)}, bf16[128,5120]{1,0:T(8,128)(2,1)}, u32[]{:S(2)}) copy-start(bf16[128,5120]{1,0:T(8,128)(2,1)} %get-tuple-element.5) | copy-start | bytes 3932164

commit v2 on v1

v2 whole, which is shorter than its diff:
```python
import math

import jax
import jax.numpy as jnp
from jax import lax
from jax.experimental import pallas as pl
from jax.experimental.pallas import tpu as pltpu
from jax.sharding import PartitionSpec as P

HD = 128
BF16 = jnp.bfloat16
F32 = jnp.float32
MESH = pl.DeviceIdType.MESH
TOK = 128
LOCAL = 384
PIECES = 5
NJ = 20
CW = 256
LAGS = (0, 1, 3, 5, 7, 9, 11)
SLOTS = 2
FLIGHT = 4


class Link:
    def __init__(self, send, recv):
        self.send, self.recv, self.used = send, recv, 0

    def take(self, n=1):
        first = self.used
        self.used += n
        return first

    def copy(self, src, dst, sem, to, send_sem=None):
        return pltpu.make_async_remote_copy(
            src_ref=src,
            dst_ref=dst,
            send_sem=self.send.at[sem if send_sem is None else send_sem],
            recv_sem=self.recv.at[sem],
            device_id=to,
            device_id_type=MESH,
        )


class Place:
    def __init__(self):
        step, head, fsdp = (lax.axis_index(a) for a in ("step", "head", "fsdp"))
        self.step, self.head = step, head
        self.y, self.x_lo, self.x_hi = step // 2, step % 2, fsdp
        self.x = self.x_hi * 2 + self.x_lo
        self.z, self.core = head // 2, head % 2

    def at(self, dx=0, dy=0, dz=0, other_core=False):
        x, y, z = (self.x + dx) % 4, (self.y + dy) % 4, (self.z + dz) % 4
        core = 1 - self.core if other_core else self.core
        return (y * 2 + x % 2, z * 2 + core, x // 2)

    def column(self, dx):
        x = (self.x + dx) % 4
        return (x % 2) * 2 + x // 2

    def row(self, dy):
        return (self.y + dy) % 4


class PlaneGather:
    def __init__(self, link, place, view, half):
        me = place
        whole, low, high = slice(0, half), slice(0, half // 2), slice(half // 2, half)
        every = slice(0, 4)
        y, c = me.y, me.column(0)
        left, right, far_x = me.column(-1), me.column(1), me.column(2)
        below, above, far_y = me.row(-1), me.row(1), me.row(2)
        east, west, north, south = me.at(dx=1), me.at(dx=-1), me.at(dy=1), me.at(dy=-1)
        self.link, self.view, self.base = link, view, link.take(16)
        self.sends = (
            ((y, c, 0, whole), east),
            ((y, c, 0, whole), west),
            ((y, c, 1, whole), north),
            ((y, c, 1, whole), south),
            ((y, left, 0, low), east),
            ((y, right, 0, high), west),
            ((below, c, 1, low), north),
            ((above, c, 1, high), south),
            ((y, every, 0, whole), north),
            ((y, every, 0, whole), south),
            ((every, c, 1, whole), east),
            ((every, c, 1, whole), west),
            ((below, every, 0, low), north),
            ((above, every, 0, high), south),
            ((every, left, 1, low), east),
            ((every, right, 1, high), west),
        )
        self.receives = (
            (y, left, 0, whole),
            (y, right, 0, whole),
            (below, c, 1, whole),
            (above, c, 1, whole),
            (y, far_x, 0, low),
            (y, far_x, 0, high),
            (far_y, c, 1, low),
            (far_y, c, 1, high),
            (below, every, 0, whole),
            (above, every, 0, whole),
            (every, left, 1, whole),
            (every, right, 1, whole),
            (far_y, every, 0, low),
            (far_y, every, 0, high),
            (every, far_x, 1, low),
            (every, far_x, 1, high),
        )

    def copy(self, slot, args):
        part = self.view(*args)
        return self.link.copy(part, part, self.base + slot, self.sends[slot][1])

    def start(self, *slots):
        for slot in slots:
            self.copy(slot, self.sends[slot][0]).start()

    def got(self, *slots):
        for slot in slots:
            self.copy(slot, self.receives[slot]).wait_recv()

    def start1(self):
        self.start(0, 1, 2, 3)

    def start2(self):
        for slot in range(4):
            self.got(slot)
            self.start(slot + 4)

    def start3(self):
        self.got(4, 5)
        self.start(8, 9)
        self.got(6, 7)
        self.start(10, 11)

    def start4(self):
        for slot in range(8, 12):
            self.got(slot)
            self.start(slot + 4)

    def finish(self):
        self.got(12, 13, 14, 15)

    def drain(self):
        for slot in range(16):
            self.copy(slot, self.sends[slot][0]).wait_send()


class TokenGather:
    def __init__(self, link, place, acts):
        self.link, self.me, self.acts = link, place, acts
        self.base = link.take(9)
        self.started = []

    def rows(self, dz, other=False, start=0, size=TOK):
        me = self.me
        z = (me.z + dz) % 4
        core = 1 - me.core if other else me.core
        return self.acts.at[pl.ds(pl.multiple_of((z * 2 + core) * TOK + start, 64), size), :]

    def go(self, slot, part, to):
        copy = self.link.copy(part, part, self.base + slot, to)
        copy.start()
        self.started.append(copy)

    def got(self, slot, part):
        self.link.copy(part, part, self.base + slot, self.me.at(dz=1)).wait_recv()

    def start1(self):
        me = self.me
        own = self.rows(0)
        self.go(0, own, me.at(dz=1))
        self.go(1, own, me.at(dz=-1))
        self.go(2, own, me.at(other_core=True))

    def start2(self):
        me = self.me
        self.got(0, self.rows(-1))
        self.go(3, self.rows(-1, size=64), me.at(dz=1))
        self.got(1, self.rows(1))
        self.go(4, self.rows(1, start=64, size=64), me.at(dz=-1))
        self.go(5, self.rows(-1), me.at(other_core=True))
        self.go(6, self.rows(1), me.at(other_core=True))

    def start3(self):
        me = self.me
        self.got(3, self.rows(2, size=64))
        self.go(7, self.rows(2, size=64), me.at(other_core=True))
        self.got(4, self.rows(2, start=64, size=64))
        self.go(8, self.rows(2, start=64, size=64), me.at(other_core=True))

    def own_chip(self):
        self.got(2, self.rows(0, other=True))

    def near_chips(self):
        self.got(5, self.rows(-1, other=True))
        self.got(6, self.rows(1, other=True))

    def far_chip(self):
        self.got(7, self.rows(2, other=True, size=64))
        self.got(8, self.rows(2, other=True, start=64, size=64))

    def drain(self):
        for copy in self.started:
            copy.wait_send()


def eye_mask():
    return lax.broadcasted_iota(jnp.int32, (128, 128), 0) == lax.broadcasted_iota(
        jnp.int32, (128, 128), 1
    )


def kernel(
    length_ref,
    time_ref,
    q_gain_ref,
    k_gain_ref,
    states_hbm,
    mod_hbm,
    wq_hbm,
    wk_hbm,
    wv_hbm,
    wo_hbm,
    next_ref,
    update_ref,
    states,
    mod,
    acts,
    w_a,
    w_b,
    w_c,
    w_d,
    w_e,
    o_full,
    raw,
    qk,
    value,
    probs,
    attended,
    squares,
    partial,
    summed,
    z_first,
    z_second,
    pair_out,
    pair_in,
    chain_out,
    chain_in,
    back_out,
    back_in,
    send_sem,
    recv_sem,
    local_sem,
):
    me = Place()
    link = Link(send_sem, recv_sem)

    barrier = pltpu.get_barrier_semaphore()
    for d in range(1, 8):
        pl.semaphore_signal(
            barrier,
            inc=1,
            device_id=(me.step, (me.head + d) % 8, me.x_hi),
            device_id_type=MESH,
        )
    for to in (me.at(dx=1), me.at(dx=-1), me.at(dy=1), me.at(dy=2), me.at(dy=3)):
        pl.semaphore_signal(barrier, inc=1, device_id=to, device_id_type=MESH)

    y, c = me.y, me.column(0)
    local = []
    for src, dst in (
        (wq_hbm.at[:, :, 0:256], w_a.at[y, c]),
        (states_hbm.at[0, 0], states),
        (mod_hbm, mod),
        (wq_hbm.at[:, :, 256:384], w_b.at[y, c, :, :, 0:128]),
        (wk_hbm.at[:, :, 0:128], w_b.at[y, c, :, :, 128:256]),
        (wk_hbm.at[:, :, 128:384], w_c.at[y, c]),
        (wv_hbm.at[:, :, 0:256], w_d.at[y, c]),
        (wv_hbm.at[:, :, 256:384], w_e.at[y, c]),
        (wo_hbm, o_full.at[:, y, c]),
    ):
        copy = pltpu.make_async_copy(src, dst, local_sem.at[len(local)])
        copy.start()
        local.append(copy)
    local[0].wait()
    pl.semaphore_wait(barrier, 12)

    def weight(full):
        return PlaneGather(link, me, lambda y, c, h, r: full.at[y, c, h, r], 160)

    def out_weight(first, last):
        return PlaneGather(link, me, lambda y, c, h, r: o_full.at[first:last, y, c, h, r], 32)

    g_a, g_b, g_c, g_d, g_e = (weight(w) for w in (w_a, w_b, w_c, w_d, w_e))
    o_a, o_b, o_c = out_weight(0, 1), out_weight(1, 2), out_weight(2, 5)
    tokens = TokenGather(link, me, acts)

    def product(rows, w):
        return jnp.dot(acts[rows, :], w[...].reshape(5120, w.shape[-1]), preferred_element_type=F32)

    def raw_product(dz, w, column):
        rows = pl.ds(pl.multiple_of(((me.z + dz) % 4) * 256, 256), 256)
        raw[rows, column * 256 : column * 256 + 256] = product(rows, w)

    with jax.named_scope("norm"):
        g_a.start1()
        for copy in local[1:]:
            copy.wait()
        g_b.start1()
        shift, scale = mod[0], 1.0 + mod[1]

        @pl.loop(0, 8)
        def _(r):
            x = states[pl.ds(pl.multiple_of(r * 16, 16), 16), :]
            centred = x - jnp.mean(x, axis=-1, keepdims=True)
            spread = jnp.mean(centred * centred, axis=-1, keepdims=True)
            out = centred * lax.rsqrt(spread + 1e-06) * scale + shift
            acts[pl.ds(pl.multiple_of(me.head * TOK + r * 16, 16), 16), :] = out.astype(BF16)

        tokens.start1()
    with jax.named_scope("a2"):
        g_a.start2()
        g_c.start1()
    with jax.named_scope("b2"):
        g_b.start2()
    with jax.named_scope("a3"):
        g_a.start3()
        g_c.start2()
    with jax.named_scope("a4"):
        g_a.start4()
        g_b.start3()
        g_d.start1()
    with jax.named_scope("a5"):
        g_a.finish()
        g_c.start3()
        g_d.start2()
        tokens.own_chip()
    with jax.named_scope("own_a"):
        raw_product(0, w_a, 0)
    with jax.named_scope("b4"):
        g_b.start4()
        g_e.start1()
    with jax.named_scope("tokens2"):
        tokens.start2()
    with jax.named_scope("b5"):
        g_b.finish()
        g_d.start3()
        g_e.start2()
    with jax.named_scope("own_b"):
        raw_product(0, w_b, 1)
    with jax.named_scope("c4"):
        g_c.start4()
        o_a.start1()
    with jax.named_scope("near_wait"):
        tokens.near_chips()
    with jax.named_scope("near_ab"):

        @pl.loop(0, 2)
        def _(i):
            raw_product(2 * i + 3, w_a, 0)
            raw_product(2 * i + 3, w_b, 1)

    with jax.named_scope("c5"):
        g_c.finish()
        g_e.start3()
        o_a.start2()
    with jax.named_scope("near_c"):

        @pl.loop(0, 3)
        def _(i):
            raw_product(i + 3, w_c, 2)

    with jax.named_scope("d4"):
        g_d.start4()
        o_b.start1()
    with jax.named_scope("tokens3"):
        tokens.start3()
    with jax.named_scope("tokens4"):
        tokens.far_chip()
    with jax.named_scope("far"):
        raw_product(2, w_a, 0)
        raw_product(2, w_b, 1)
        raw_product(2, w_c, 2)
    with jax.named_scope("squares"):

        @pl.loop(0, 8)
        def _(b):
            rows = pl.ds(pl.multiple_of(b * 128, 128), 128)
            for part in range(2):
                p = raw[rows, part * LOCAL : (part + 1) * LOCAL]
                total = jnp.sum(p * p, axis=1, keepdims=True)
                row = jnp.sum(jnp.where(eye_mask(), total, 0.0), axis=0, keepdims=True)
                squares[me.head, pl.ds(part * 8 + b, 1), :] = row

        base = link.take(7)
        sent = []
        for d in range(1, 8):
            own = squares.at[me.head]
            copy = link.copy(own, own, base + d - 1, (me.step, (me.head + d) % 8, me.x_hi))
            copy.start()
            sent.append(copy)
    length = length_ref[0]

    def softmax(h, m):
        rows = pl.ds(pl.multiple_of(m * 256, 256), 256)
        valid = lax.broadcasted_iota(jnp.int32, (256, 1024), 1) < length
        q = qk[rows, h * HD : (h + 1) * HD]
        k = qk[:, LOCAL + h * HD : LOCAL + (h + 1) * HD]
        s = lax.dot_general(q, k, (((1,), (1,)), ((), ())), preferred_element_type=F32)
        s = jnp.where(valid, s * (math.log2(math.e) / math.sqrt(HD)), -jnp.inf)
        e = jnp.exp2(s - jnp.max(s, axis=-1, keepdims=True))
        probs[h, rows, :] = (e * (1.0 / jnp.sum(e, axis=-1, keepdims=True))).astype(BF16)

    def attend(h, m):
        rows = pl.ds(pl.multiple_of(m * 256, 256), 256)
        o = jnp.dot(probs[h, rows, :], value[:, h * HD : (h + 1) * HD], preferred_element_type=F32)
        attended[rows, h * HD : (h + 1) * HD] = o.astype(BF16)

    def value_product(w, cols, m):
        rows = pl.ds(pl.multiple_of(m * 256, 256), 256)
        value[rows, cols] = product(rows, w).astype(BF16)

    with jax.named_scope("e4"):
        g_e.start4()
        o_a.start3()
        o_b.start2()
    with jax.named_scope("d5"):
        g_d.finish()
        o_c.start1()
    with jax.named_scope("value_d"):

        @pl.loop(0, 4)
        def _(m):
            value_product(w_d, slice(0, 256), m)

    with jax.named_scope("squares_wait"):
        for d in range(1, 8):
            theirs = squares.at[(me.head - d) % 8]
            link.copy(theirs, theirs, base + d - 1, (me.step, (me.head + d) % 8, me.x_hi)).wait_recv()
        for copy in sent:
            copy.wait_send()

    with jax.named_scope("qk_norm"):

        @pl.loop(0, 8)
        def _(b):
            rows = pl.ds(pl.multiple_of(b * 128, 128), 128)
            for part, gain in enumerate((q_gain_ref, k_gain_ref)):
                total = squares[0, pl.ds(part * 8 + b, 1), :]
                for d in range(1, 8):
                    total = total + squares[d, pl.ds(part * 8 + b, 1), :]
                factor = lax.rsqrt(total / 3072.0 + 1e-06)
                column = jnp.sum(jnp.where(eye_mask(), factor, 0.0), axis=1, keepdims=True)
                cols = slice(part * LOCAL, (part + 1) * LOCAL)
                qk[rows, cols] = (raw[rows, cols] * column * gain[...].reshape(1, LOCAL)).astype(BF16)

    with jax.named_scope("softmax0"):

        @pl.loop(0, 4)
        def _(m):
            softmax(0, m)

    with jax.named_scope("o_a4"):
        o_a.start4()
        o_b.start3()
        o_c.start2()
    with jax.named_scope("e5"):
        g_e.finish()
    with jax.named_scope("softmax1_value_e"):

        @pl.loop(0, 4)
        def _(m):
            softmax(1, m)
            value_product(w_e, slice(256, 384), m)

    with jax.named_scope("o_b4"):
        o_b.start4()
        o_c.start3()
    with jax.named_scope("softmax2_attend0"):

        @pl.loop(0, 4)
        def _(m):
            softmax(2, m)
            attend(0, m)

    with jax.named_scope("attend12"):

        @pl.loop(0, 4)
        def _(m):
            attend(1, m)
            attend(2, m)

    with jax.named_scope("o_a5"):
        o_a.finish()
        for g in (g_a, g_b, g_c, g_d, g_e, tokens):
            g.drain()

    sending = link.used
    sib, first, second = link.take(NJ), link.take(2 * NJ), link.take(2 * NJ)
    pair, chain, back = link.take(NJ), link.take(3 * NJ), link.take(NJ)
    up, down = me.at(dz=1), me.at(dz=-1)
    above, below, far = (me.z + 1) % 4, (me.z - 1) % 4, (me.z + 2) % 4
    partner = (me.y * 2 + 1 - me.x_lo, me.head, me.x_hi)
    later = [me.at(dy=d) for d in (1, 2, 3)]
    on_low = me.x_lo == 0
    lower = lax.broadcasted_iota(jnp.int32, (TOK, 128), 1) < 64
    width = (jnp.full((1, 128), time_ref[0, 1] - time_ref[0, 0], jnp.int32)).astype(F32) / 1000.0

    def turn(j, kind):
        return sending + kind * FLIGHT + j % FLIGHT

    def sib_copy(j):
        return link.copy(
            partial.at[j % SLOTS, :, 1 - me.core], summed.at[j], sib + j, me.at(other_core=True), turn(j, 0)
        )

    def first_copies(j):
        return (
            link.copy(summed.at[j, far, 0:64], z_first.at[j, 0], first + 2 * j, up, turn(j, 1)),
            link.copy(summed.at[j, far, 64:128], z_first.at[j, 1], first + 2 * j + 1, down, turn(j, 2)),
        )

    def second_copies(j):
        return (
            link.copy(summed.at[j, above], z_second.at[j, 0], second + 2 * j, up, turn(j, 3)),
            link.copy(summed.at[j, below], z_second.at[j, 1], second + 2 * j + 1, down, turn(j, 4)),
        )

    def pair_copy(j):
        return link.copy(pair_out.at[j], pair_in.at[j], pair + j, partner, turn(j, 5))

    def chain_copy(j, d):
        return link.copy(
            chain_out.at[j], chain_in.at[j, d - 1], chain + 3 * j + d - 1, later[d - 1], turn(j, 6 + d)
        )

    def back_copy(j):
        return link.copy(back_out.at[j], back_in.at[j], back + j, partner, turn(j, 6))

    def natural(j, m):
        piece, tile = j // 4, (j % 4) * 2 + m
        odd = piece % 2
        low = 5 * tile + (piece + 5 * odd) // 2
        high = 5 * tile + 2 * (1 - odd) + (piece - odd) // 2
        return (
            pl.ds(pl.multiple_of(low * 128, 128), 128),
            pl.ds(pl.multiple_of(high * 128, 128), 128),
        )

    def kept(j, half):
        start = (j % 8) * 128 + half * 64
        return pl.ds(pl.multiple_of(start, 64), 64), pl.ds(pl.multiple_of((j // 8) * 256, 256), 256)

    def project(j):
        w = o_full[j // 4, j % 4].reshape(CW, LOCAL)
        for m in range(4):
            p = lax.dot_general(
                attended[m * 256 : (m + 1) * 256, :],
                w,
                (((1,), (1,)), ((), ())),
                preferred_element_type=F32,
            ).astype(BF16)
            partial[j % SLOTS, m, 0] = p[0:128]
            partial[j % SLOTS, m, 1] = p[128:256]
        sib_copy(j).start()

    def add_sibling(j):
        copy = sib_copy(j)
        copy.wait_recv()
        for m in range(4):
            own = partial[j % SLOTS, m, me.core].astype(F32)
            summed[j, m] = (own + summed[j, m].astype(F32)).astype(BF16)
        copy.wait_send()
        for c in first_copies(j):
            c.start()

    def add_far(j):
        copies = first_copies(j)
        for c in copies:
            c.wait_recv()
        summed[j, above, 0:64] = (
            summed[j, above, 0:64].astype(F32) + z_first[j, 0].astype(F32)
        ).astype(BF16)
        summed[j, below, 64:128] = (
            summed[j, below, 64:128].astype(F32) + z_first[j, 1].astype(F32)
        ).astype(BF16)
        for c in second_copies(j):
            c.start()
        for c in copies:
            c.wait_send()

    def drift(j):
        copies = second_copies(j)
        for c in copies:
            c.wait_recv()
        rows = pl.ds(pl.multiple_of((j % 8) * 128, 128), 128)
        for m in range(2):
            lanes = slice(m * 128, (m + 1) * 128)
            total = (
                summed[j, me.z, :, lanes].astype(F32)
                + z_second[j, 0, :, lanes].astype(F32)
                + z_second[j, 1, :, lanes].astype(F32)
            )
            projected = jnp.where((j // 4) % 2 == 1, pltpu.roll(total, 64, 1), total)
            low, high = natural(j, m)
            gate = jnp.where(lower[0:1], mod[2, :, low], mod[2, :, high])
            branch = gate * projected
            update_ref[:, low] = jnp.where(lower, branch, update_ref[:, low].astype(F32)).astype(BF16)
            update_ref[:, high] = jnp.where(lower, update_ref[:, high].astype(F32), branch).astype(BF16)
            current = jnp.where(lower, states[:, low], states[:, high])
            anchor = jnp.where(me.step == 0, current, 0.0)
            raw[rows, pl.ds(pl.multiple_of((j // 8) * 256 + m * 128, 128), 128)] = (
                width * (current + branch) + anchor
            )
        pair_out[j] = raw[kept(j, 1 - me.x_lo)].astype(BF16)
        pair_copy(j).start()
        for c in copies:
            c.wait_send()

    def add_pair(j):
        copy = pair_copy(j)
        copy.wait_recv()
        chain_out[j] = (raw[kept(j, me.x_lo)] + pair_in[j].astype(F32)).astype(BF16)
        for d in (1, 2, 3):

            @pl.when(me.y + d < 4)
            def _(d=d):
                chain_copy(j, d).start()

        copy.wait_send()

    def add_earlier(j):
        for d in (1, 2, 3):

            @pl.when(me.y >= d)
            def _(d=d):
                chain_copy(j, d).wait_recv()

        earlier = jnp.zeros((64, CW), F32)
        for d in (1, 2, 3):
            earlier = earlier + jnp.where(me.y >= d, chain_in[j, d - 1].astype(F32), 0.0)
        mine = kept(j, me.x_lo)
        own = raw[mine]
        back_out[j] = (earlier + jnp.where(on_low, own, 0.0)).astype(BF16)
        back_copy(j).start()
        raw[mine] = own + (earlier + jnp.where(on_low, 0.0, pair_in[j].astype(F32)))
        for d in (1, 2, 3):

            @pl.when(me.y + d < 4)
            def _(d=d):
                chain_copy(j, d).wait_send()

    def add_back(j):
        copy = back_copy(j)
        copy.wait_recv()
        other = kept(j, 1 - me.x_lo)
        raw[other] = raw[other] + back_in[j].astype(F32)
        rows = pl.ds(pl.multiple_of((j % 8) * 128, 128), 128)
        for m in range(2):
            low, high = natural(j, m)
            total = raw[rows, pl.ds(pl.multiple_of((j // 8) * 256 + m * 128, 128), 128)]
            next_ref[:, low] = jnp.where(lower, total, next_ref[:, low])
            next_ref[:, high] = jnp.where(lower, next_ref[:, high], total)
        copy.wait_send()

    with jax.named_scope("reduce"):
        stages = (project, add_sibling, add_far, drift, add_pair, add_earlier, add_back)

        @pl.loop(0, NJ + LAGS[-1])
        def _(i):
            @pl.when(i == 2)
            def _():
                o_c.start4()

            @pl.when(i == 4)
            def _():
                o_b.finish()

            @pl.when(i == 8)
            def _():
                o_c.finish()

            for lag, stage in zip(LAGS, stages):
                j = i - lag

                @pl.when((j >= 0) & (j < NJ))
                def _(stage=stage, j=j):
                    stage(j)

    for g in (o_a, o_b, o_c):
        g.drain()


def body(states, timesteps, lengths, modulation, w_query, w_key, w_value, w_out, q_gain, k_gain):
    n_gather = 8 * 16 + 9 + 7
    vmem = pl.BlockSpec(memory_space=pltpu.VMEM)
    smem = pl.BlockSpec(memory_space=pltpu.SMEM)
    anywhere = pl.BlockSpec(memory_space=pl.ANY)
    nxt, update = pl.pallas_call(
        kernel,
        out_shape=(
            jax.ShapeDtypeStruct((TOK, 5120), F32),
            jax.ShapeDtypeStruct((TOK, 5120), BF16),
        ),
        in_specs=[smem, smem, vmem, vmem] + [anywhere] * 6,
        out_specs=(vmem, vmem),
        scratch_shapes=[
            pltpu.VMEM((TOK, 5120), F32),
            pltpu.VMEM((3, 1, 5120), F32),
            pltpu.VMEM((1024, 5120), BF16),
            pltpu.VMEM((4, 4, 2, 160, 256), BF16),
            pltpu.VMEM((4, 4, 2, 160, 256), BF16),
            pltpu.VMEM((4, 4, 2, 160, 256), BF16),
            pltpu.VMEM((4, 4, 2, 160, 256), BF16),
            pltpu.VMEM((4, 4, 2, 160, 128), BF16),
            pltpu.VMEM((PIECES, 4, 4, 2, 32, LOCAL), BF16),
            pltpu.VMEM((1024, 2 * LOCAL), F32),
            pltpu.VMEM((1024, 2 * LOCAL), BF16),
            pltpu.VMEM((1024, LOCAL), BF16),
            pltpu.VMEM((3, 1024, 1024), BF16),
            pltpu.VMEM((1024, LOCAL), BF16),
            pltpu.VMEM((8, 16, 128), F32),
            pltpu.VMEM((SLOTS, 4, 2, TOK, CW), BF16),
            pltpu.VMEM((NJ, 4, TOK, CW), BF16),
            pltpu.VMEM((NJ, 2, 64, CW), BF16),
            pltpu.VMEM((NJ, 2, TOK, CW), BF16),
            pltpu.VMEM((NJ, 64, CW), BF16),
            pltpu.VMEM((NJ, 64, CW), BF16),
            pltpu.VMEM((NJ, 64, CW), BF16),
            pltpu.VMEM((NJ, 3, 64, CW), BF16),
            pltpu.VMEM((NJ, 64, CW), BF16),
            pltpu.VMEM((NJ, 64, CW), BF16),
            pltpu.SemaphoreType.DMA((n_gather + 10 * FLIGHT,)),
            pltpu.SemaphoreType.DMA((n_gather + 10 * NJ,)),
            pltpu.SemaphoreType.DMA((9,)),
        ],
        compiler_params=pltpu.CompilerParams(
            collective_id=0,
            has_side_effects=True,
            vmem_limit_bytes=63 * 1024 * 1024,
        ),
    )(
        lengths,
        timesteps,
        q_gain,
        k_gain,
        states,
        modulation.transpose(1, 0, 2),
        w_query.reshape(2, 160, LOCAL),
        w_key.reshape(2, 160, LOCAL),
        w_value.reshape(2, 160, LOCAL),
        w_out.T.reshape(PIECES, 2, 32, LOCAL),
    )
    return (nxt[None, None], update[None, None])


def solution(mesh):
    in_specs = (
        P("step", "fsdp", "head", None),
        P("step", None),
        P("fsdp"),
        P("step", None, None),
        P(("step", "fsdp"), "head"),
        P(("step", "fsdp"), "head"),
        P(("step", "fsdp"), "head"),
        P("head", ("step", "fsdp")),
        P("head"),
        P("head"),
    )
    out_specs = (P("step", "fsdp", "head", None), P("step", "fsdp", "head", None))
    return jax.shard_map(body, mesh=mesh, in_specs=in_specs, out_specs=out_specs, check_vma=False)
```

time: 183 us -> 162 us (0.89)
  Pallas kernels: 169 us -> 156 us
  local copies, waits for them, and re-layouts: 8.81 us -> 4.65 us
  other arithmetic: 2.47 us -> 0 us
    pallas_call x1, Pallas kernels: 169 us -> 156 us  [body(): pl.pallas_call(kernel, out_shape=(jax.ShapeDtypeStruct((TOK, 5120), F32),...]
    concatenate x1 -> x0, other arithmetic: 1.88 us -> none  [body(): jnp.concatenate([w_query, w_key], axis=1)]
    unnamed x5 -> x4, local copies, waits for them, and re-layouts: 6.13 us -> 4.65 us
where the time goes in v2:
time: 162 us
  Pallas kernels  156 us (96%)
  local copies, waits for them, and re-layouts  4.65 us (3%)
    pallas_call x1, Pallas kernels, body(): pl.pallas_call(kernel, out_shape=(jax.ShapeDtypeStruct((TOK, 5120), F32),...  156 us
    unnamed x4, local copies, waits for them, and re-layouts  4.65 us

profile of v2, /device:TPU:24, one launch (start us, length us, event | category | flops | bytes accessed | tf_op | source)
XLA Modules:
  0.0 161.5 jit_solution(17788523677080185497)
XLA Ops:
  1.3 155.6 %shard_map.113 = (f32[128,5120]{1,0:T(8,128)}, bf16[128,5120]{1,0:T(8,128)(2,1)}) custom-call(s32[1]{0:T(128)S(6)} %copy.14.length_ref, s32[1,2]{1,0:T(1,128)} %time_ref.1, f32[384]{0:T(512)} %q_gain_ref.1, f32[384]{0:T(512)} %k_gain_ref.1, f32[1,1,128,5120]{3,2,1,0:T(8,128)} %states_hbm.1, f32[3,1,5120]{2,1,0:T(1,128)} %bitcast.15, ...), custom_call_target="tpu_custom_call" | custom-call | tf_op jit(solution)/shard_map/pallas_call | solution.py:702
  156.8 0.0 copy-start
  156.9 3.6 %copy.15 = f32[1,1,128,5120]{3,2,1,0:T(8,128)} copy(f32[1,1,128,5120]{3,2,1,0:T(8,128)} %bitcast.9) | data formatting | bytes 5242880
  160.4 0.0 copy-done
  160.4 1.1 copy.16
Async XLA Ops:
  156.8 3.6 %copy-start = (bf16[128,5120]{1,0:T(8,128)(2,1)S(1)}, bf16[128,5120]{1,0:T(8,128)(2,1)}, u32[]{:S(2)}) copy-start(bf16[128,5120]{1,0:T(8,128)(2,1)} %get-tuple-element.5) | copy-start | bytes 3932164

commit v3 on v2

v3 whole, which is shorter than its diff:
```python
import math

import jax
import jax.numpy as jnp
from jax import lax
from jax.experimental import pallas as pl
from jax.experimental.pallas import tpu as pltpu
from jax.sharding import PartitionSpec as P

HD = 128
BF16 = jnp.bfloat16
F32 = jnp.float32
MESH = pl.DeviceIdType.MESH
TOK = 128
LOCAL = 384
PIECES = 5
NJ = 20
CW = 256
LAGS = (0, 1, 3, 5, 7, 9, 11)
SLOTS = 2
FLIGHT = 4
AHEAD = 8


class Link:
    def __init__(self, send, recv, some_device):
        self.send, self.recv, self.to = send, recv, some_device
        self.sends, self.recvs = 0, 0

    def take(self, sends, recvs):
        first = self.sends, self.recvs
        self.sends, self.recvs = self.sends + sends, self.recvs + recvs
        return first

    def copy(self, src, dst, send, recv, to):
        return pltpu.make_async_remote_copy(
            src_ref=src,
            dst_ref=dst,
            send_sem=self.send.at[send],
            recv_sem=self.recv.at[recv],
            device_id=to,
            device_id_type=MESH,
        )

    def sent(self, send, size):
        self.copy(size, size, send, 0, self.to).wait_send()

    def got(self, recv, size):
        self.copy(size, size, 0, recv, self.to).wait_recv()


class Place:
    def __init__(self):
        step, head, fsdp = (lax.axis_index(a) for a in ("step", "head", "fsdp"))
        self.step, self.head = step, head
        self.y, self.x_lo, self.x_hi = step // 2, step % 2, fsdp
        self.x = self.x_hi * 2 + self.x_lo
        self.z, self.core = head // 2, head % 2

    def at(self, dx=0, dy=0, dz=0, other_core=False):
        x, y, z = (self.x + dx) % 4, (self.y + dy) % 4, (self.z + dz) % 4
        core = 1 - self.core if other_core else self.core
        return (y * 2 + x % 2, z * 2 + core, x // 2)

    def column(self, dx):
        x = (self.x + dx) % 4
        return (x % 2) * 2 + x // 2

    def row(self, dy):
        return (self.y + dy) % 4


class PlaneGather:
    def __init__(self, link, place, view, half):
        me = place
        whole, low, high = slice(0, half), slice(0, half // 2), slice(half // 2, half)
        every = slice(0, 4)
        y, c = me.y, me.column(0)
        left, right, far_x = me.column(-1), me.column(1), me.column(2)
        below, above, far_y = me.row(-1), me.row(1), me.row(2)
        east, west, north, south = me.at(dx=1), me.at(dx=-1), me.at(dy=1), me.at(dy=-1)
        self.link, self.view = link, view
        self.s, self.r = link.take(4, 6)
        self.sends = (
            ((y, c, 0, whole), east),
            ((y, c, 0, whole), west),
            ((y, c, 1, whole), north),
            ((y, c, 1, whole), south),
            ((y, left, 0, low), east),
            ((y, right, 0, high), west),
            ((below, c, 1, low), north),
            ((above, c, 1, high), south),
            ((y, every, 0, whole), north),
            ((y, every, 0, whole), south),
            ((every, c, 1, whole), east),
            ((every, c, 1, whole), west),
            ((below, every, 0, low), north),
            ((above, every, 0, high), south),
            ((every, left, 1, low), east),
            ((every, right, 1, high), west),
        )
        two = slice(0, 2)
        self.pair = view(y, two, 0, whole)
        self.rows = view(two, every, 0, whole)
        self.half = view(every, every, 0, whole)
        self.row = view(y, every, 0, whole)

    def start(self, first, last):
        for slot in range(first, last):
            args, to = self.sends[slot]
            part = self.view(*args)
            recv = (0, 0, 1, 1, 2, 2, 2, 2, 3, 3, 4, 4, 5, 5, 5, 5)[slot]
            self.link.copy(part, part, self.s + slot // 4, self.r + recv, to).start()

    def got(self, n, size):
        self.link.got(self.r + n, size)

    def start1(self):
        self.start(0, 4)

    def start2(self):
        self.got(0, self.pair)
        self.start(4, 6)
        self.got(1, self.pair)
        self.start(6, 8)

    def start3(self):
        self.got(2, self.pair)
        self.start(8, 12)

    def start4(self):
        self.got(3, self.rows)
        self.start(12, 14)
        self.got(4, self.rows)
        self.start(14, 16)

    def finish(self):
        self.got(5, self.rows)

    def drain(self):
        for phase, size in enumerate((self.row, self.pair, self.half, self.rows)):
            self.link.sent(self.s + phase, size)


class TokenGather:
    def __init__(self, link, place, acts):
        self.link, self.me, self.acts = link, place, acts
        self.s, self.r = link.take(6, 6)

    def rows(self, dz, start=0, size=TOK):
        me = self.me
        z = (me.z + dz) % 4
        return self.acts.at[pl.ds(pl.multiple_of((z * 2 + me.core) * TOK + start, 64), size), :]

    def low(self, dz):
        return self.rows(dz, 0, 64)

    def high(self, dz):
        return self.rows(dz, 64, 64)

    def go(self, n, part, to):
        self.link.copy(part, part, self.s + n, self.r + n, to).start()

    def got(self, n, rows=TOK):
        self.link.got(self.r + n, self.acts.at[0:rows])

    def start1(self):
        up, down = self.me.at(dz=1), self.me.at(dz=-1)
        self.go(0, self.low(0), up)
        self.go(0, self.high(0), down)
        self.go(1, self.high(0), up)
        self.go(1, self.low(0), down)
        self.go(2, self.rows(0), self.me.at(other_core=True))

    def start2(self):
        self.got(0)
        self.go(3, self.low(-1), self.me.at(dz=1))
        self.go(3, self.high(1), self.me.at(dz=-1))

    def start3(self):
        other = self.me.at(other_core=True)
        self.got(1)
        self.go(4, self.rows(-1), other)
        self.go(4, self.rows(1), other)

    def start4(self):
        self.got(3)
        self.go(5, self.rows(2), self.me.at(other_core=True))

    def own_chip(self):
        self.got(2)

    def near_chips(self):
        self.got(4, 2 * TOK)

    def far_chip(self):
        self.got(5)

    def drain(self):
        for n in range(6):
            self.link.sent(self.s + n, self.acts.at[0 : 2 * TOK if n == 4 else TOK])


def eye_mask():
    return lax.broadcasted_iota(jnp.int32, (128, 128), 0) == lax.broadcasted_iota(
        jnp.int32, (128, 128), 1
    )


def kernel(
    length_ref,
    time_ref,
    q_gain_ref,
    k_gain_ref,
    states_hbm,
    mod_hbm,
    wq_hbm,
    wk_hbm,
    wv_hbm,
    wo_hbm,
    next_hbm,
    update_hbm,
    states,
    mod,
    acts,
    w_a,
    w_b,
    w_c,
    w_d,
    w_e,
    o_full,
    raw,
    qk,
    value,
    probs,
    attended,
    squares,
    partial,
    summed,
    z_first,
    z_second,
    pair_out,
    pair_in,
    chain_out,
    chain_in,
    back_out,
    back_in,
    send_sem,
    recv_sem,
    local_sem,
):
    me = Place()
    link = Link(send_sem, recv_sem, me.at(dx=1))

    barrier = pltpu.get_barrier_semaphore()
    for d in range(1, 8):
        pl.semaphore_signal(
            barrier,
            inc=1,
            device_id=(me.step, (me.head + d) % 8, me.x_hi),
            device_id_type=MESH,
        )
    for to in [me.at(dx=1), me.at(dx=-1)] + [me.at(dy=d) for d in (1, 2, 3)]:
        pl.semaphore_signal(barrier, inc=1, device_id=to, device_id_type=MESH)

    y, c = me.y, me.column(0)
    local = []
    for src, dst in (
        (states_hbm.at[0, 0], states),
        (mod_hbm, mod),
        (wq_hbm.at[:, :, 0:256], w_a.at[y, c]),
        (wq_hbm.at[:, :, 256:384], w_b.at[y, c, :, :, 0:128]),
        (wk_hbm.at[:, :, 0:128], w_b.at[y, c, :, :, 128:256]),
        (wk_hbm.at[:, :, 128:384], w_c.at[y, c]),
        (wv_hbm.at[:, :, 0:256], w_d.at[y, c]),
        (wv_hbm.at[:, :, 256:384], w_e.at[y, c]),
        (wo_hbm, o_full.at[:, y, c]),
    ):
        copy = pltpu.make_async_copy(src, dst, local_sem.at[len(local)])
        copy.start()
        local.append(copy)

    def weight(full):
        return PlaneGather(link, me, lambda y, c, h, r: full.at[y, c, h, r], 160)

    def out_weight(first, last):
        return PlaneGather(link, me, lambda y, c, h, r: o_full.at[first:last, y, c, h, r], 32)

    g_a, g_b, g_c, g_d, g_e = (weight(w) for w in (w_a, w_b, w_c, w_d, w_e))
    o_a, o_b, o_c = out_weight(0, 1), out_weight(1, 2), out_weight(2, 5)
    tokens = TokenGather(link, me, acts)

    def product(rows, w):
        return jnp.dot(acts[rows, :], w[...].reshape(5120, w.shape[-1]), preferred_element_type=F32)

    def raw_product(dz, w, column):
        rows = pl.ds(pl.multiple_of(((me.z + dz) % 4) * 256, 256), 256)
        raw[rows, column * 256 : column * 256 + 256] = product(rows, w)

    with jax.named_scope("norm"):
        local[0].wait()
        local[1].wait()
        shift, scale = mod[0], 1.0 + mod[1]

        @pl.loop(0, 4)
        def _(r):
            x = states[pl.ds(pl.multiple_of(r * 32, 32), 32), :]
            centred = x - jnp.mean(x, axis=-1, keepdims=True)
            spread = jnp.mean(centred * centred, axis=-1, keepdims=True)
            out = centred * lax.rsqrt(spread + 1e-06) * scale + shift
            acts[pl.ds(pl.multiple_of(me.head * TOK + r * 32, 32), 32), :] = out.astype(BF16)

    with jax.named_scope("barrier"):
        local[2].wait()
        pl.semaphore_wait(barrier, 12)
    with jax.named_scope("a1"):
        g_a.start1()
        tokens.start1()
        for copy in local[3:]:
            copy.wait()
        g_b.start1()
    with jax.named_scope("a2"):
        g_a.start2()
        g_c.start1()
    with jax.named_scope("b2"):
        g_b.start2()
    with jax.named_scope("a3"):
        g_a.start3()
    with jax.named_scope("a4"):
        g_a.start4()
        g_c.start2()
        g_b.start3()
        g_d.start1()
    with jax.named_scope("tokens2"):
        tokens.start2()
    with jax.named_scope("a5"):
        g_a.finish()
        tokens.own_chip()
    with jax.named_scope("own_a"):
        raw_product(0, w_a, 0)
    with jax.named_scope("b4"):
        g_b.start4()
        g_d.start2()
        g_c.start3()
        g_e.start1()
    with jax.named_scope("tokens3"):
        tokens.start3()
    with jax.named_scope("b5"):
        g_b.finish()
    with jax.named_scope("own_b"):
        raw_product(0, w_b, 1)
    with jax.named_scope("near_wait"):
        tokens.near_chips()
    with jax.named_scope("near_ab"):

        @pl.loop(0, 2)
        def _(i):
            raw_product(2 * i + 3, w_a, 0)
            raw_product(2 * i + 3, w_b, 1)

    with jax.named_scope("c4"):
        g_c.start4()
        g_e.start2()
        g_d.start3()
        o_a.start1()
    with jax.named_scope("tokens4"):
        tokens.start4()
    with jax.named_scope("c5"):
        g_c.finish()
    with jax.named_scope("near_c"):

        @pl.loop(0, 3)
        def _(i):
            raw_product(i + 3, w_c, 2)

    with jax.named_scope("far_wait"):
        tokens.far_chip()
    with jax.named_scope("far"):
        raw_product(2, w_a, 0)
        raw_product(2, w_b, 1)
        raw_product(2, w_c, 2)
    with jax.named_scope("squares"):

        @pl.loop(0, 8)
        def _(b):
            rows = pl.ds(pl.multiple_of(b * 128, 128), 128)
            for part in range(2):
                p = raw[rows, part * LOCAL : (part + 1) * LOCAL]
                total = jnp.sum(p * p, axis=1, keepdims=True)
                row = jnp.sum(jnp.where(eye_mask(), total, 0.0), axis=0, keepdims=True)
                squares[me.head, pl.ds(part * 8 + b, 1), :] = row

        s_squares, r_squares = link.take(1, 1)
        for d in range(1, 8):
            own = squares.at[me.head]
            to = (me.step, (me.head + d) % 8, me.x_hi)
            link.copy(own, own, s_squares, r_squares, to).start()
    length = length_ref[0]

    def softmax(h, m):
        rows = pl.ds(pl.multiple_of(m * 256, 256), 256)
        valid = lax.broadcasted_iota(jnp.int32, (256, 1024), 1) < length
        q = qk[rows, h * HD : (h + 1) * HD]
        k = qk[:, LOCAL + h * HD : LOCAL + (h + 1) * HD]
        s = lax.dot_general(q, k, (((1,), (1,)), ((), ())), preferred_element_type=F32)
        s = jnp.where(valid, s * (math.log2(math.e) / math.sqrt(HD)), -jnp.inf)
        e = jnp.exp2(s - jnp.max(s, axis=-1, keepdims=True))
        probs[h, rows, :] = (e * (1.0 / jnp.sum(e, axis=-1, keepdims=True))).astype(BF16)

    def attend(h, m):
        rows = pl.ds(pl.multiple_of(m * 256, 256), 256)
        o = jnp.dot(probs[h, rows, :], value[:, h * HD : (h + 1) * HD], preferred_element_type=F32)
        attended[rows, h * HD : (h + 1) * HD] = o.astype(BF16)

    def value_product(w, cols, m):
        rows = pl.ds(pl.multiple_of(m * 256, 256), 256)
        value[rows, cols] = product(rows, w).astype(BF16)

    with jax.named_scope("d4"):
        g_d.start4()
        o_a.start2()
        g_e.start3()
        o_b.start1()
        o_c.start1()
    with jax.named_scope("squares_wait"):
        link.got(r_squares, squares.at[0:7])
        link.sent(s_squares, squares.at[0:7])

    with jax.named_scope("qk_norm"):

        @pl.loop(0, 8)
        def _(b):
            rows = pl.ds(pl.multiple_of(b * 128, 128), 128)
            for part, gain in enumerate((q_gain_ref, k_gain_ref)):
                total = squares[0, pl.ds(part * 8 + b, 1), :]
                for d in range(1, 8):
                    total = total + squares[d, pl.ds(part * 8 + b, 1), :]
                factor = lax.rsqrt(total / 3072.0 + 1e-06)
                column = jnp.sum(jnp.where(eye_mask(), factor, 0.0), axis=1, keepdims=True)
                cols = slice(part * LOCAL, (part + 1) * LOCAL)
                qk[rows, cols] = (raw[rows, cols] * column * gain[...].reshape(1, LOCAL)).astype(BF16)

    with jax.named_scope("softmax0"):

        @pl.loop(0, 4)
        def _(m):
            softmax(0, m)

    with jax.named_scope("o_a3"):
        o_a.start3()
    with jax.named_scope("softmax1"):

        @pl.loop(0, 4)
        def _(m):
            softmax(1, m)

    with jax.named_scope("d5"):
        g_d.finish()
    with jax.named_scope("e4"):
        g_e.start4()
        o_b.start2()
        o_c.start2()
    with jax.named_scope("value_d"):

        @pl.loop(0, 4)
        def _(m):
            value_product(w_d, slice(0, 256), m)

    with jax.named_scope("o_b3"):
        o_a.start4()
        o_b.start3()
    with jax.named_scope("softmax2"):

        @pl.loop(0, 4)
        def _(m):
            softmax(2, m)

    with jax.named_scope("attend01"):

        @pl.loop(0, 4)
        def _(m):
            attend(0, m)
            attend(1, m)

    with jax.named_scope("e5"):
        g_e.finish()
        o_c.start3()
    with jax.named_scope("value_e"):

        @pl.loop(0, 4)
        def _(m):
            value_product(w_e, slice(256, 384), m)

    with jax.named_scope("o_b4"):
        o_b.start4()
    with jax.named_scope("attend2"):

        @pl.loop(0, 4)
        def _(m):
            attend(2, m)

    with jax.named_scope("o_a5"):
        o_a.finish()
        for g in (g_a, g_b, g_c, g_d, g_e, tokens):
            g.drain()

    kinds = [link.take(FLIGHT, NJ if kind == 4 else AHEAD) for kind in range(6)]
    sib, first, second, pair, chain, back = range(6)
    up, down = me.at(dz=1), me.at(dz=-1)
    above, below, far = (me.z + 1) % 4, (me.z - 1) % 4, (me.z + 2) % 4
    partner = (me.y * 2 + 1 - me.x_lo, me.head, me.x_hi)
    later = [me.at(dy=d) for d in (1, 2, 3)]
    on_low = me.x_lo == 0
    lower = lax.broadcasted_iota(jnp.int32, (TOK, 128), 1) < 64
    width = (jnp.full((1, 128), time_ref[0, 1] - time_ref[0, 0], jnp.int32)).astype(F32) / 1000.0

    def send_of(kind, j):
        return kinds[kind][0] + j % FLIGHT

    def recv_of(kind, j):
        return kinds[kind][1] + (j if kind == chain else j % AHEAD)

    def go(kind, j, src, dst, to):
        link.copy(src, dst, send_of(kind, j), recv_of(kind, j), to).start()

    def got(kind, j, size):
        link.got(recv_of(kind, j), size)

    def sent(kind, j, size):
        link.sent(send_of(kind, j), size)

    def quarter(n):
        return pl.ds(pl.multiple_of(n * 1280, 128), 1280)

    def next_out(n):
        return pltpu.make_async_copy(states.at[:, quarter(n)], next_hbm.at[:, quarter(n)], local_sem.at[n])

    def update_out(n):
        return pltpu.make_async_copy(
            acts.at[0:TOK, quarter(n)], update_hbm.at[:, quarter(n)], local_sem.at[4 + n]
        )

    def natural(j, m):
        piece, tile = j // 4, (j % 4) * 2 + m
        odd = piece % 2
        low = 5 * tile + (piece + 5 * odd) // 2
        high = 5 * tile + 2 * (1 - odd) + (piece - odd) // 2
        return (
            pl.ds(pl.multiple_of(low * 128, 128), 128),
            pl.ds(pl.multiple_of(high * 128, 128), 128),
        )

    def kept(j, half):
        start = (j % 8) * 128 + half * 64
        return pl.ds(pl.multiple_of(start, 64), 64), pl.ds(pl.multiple_of((j // 8) * 256, 256), 256)

    def project(j):
        w = o_full[j // 4, j % 4].reshape(CW, LOCAL)
        for m in range(4):
            p = lax.dot_general(
                attended[m * 256 : (m + 1) * 256, :],
                w,
                (((1,), (1,)), ((), ())),
                preferred_element_type=F32,
            ).astype(BF16)
            partial[j % SLOTS, m, 0] = p[0:128]
            partial[j % SLOTS, m, 1] = p[128:256]
        go(sib, j, partial.at[j % SLOTS, :, 1 - me.core], summed.at[j], me.at(other_core=True))

    def add_sibling(j):
        got(sib, j, summed.at[j])
        for m in range(4):
            own = partial[j % SLOTS, m, me.core].astype(F32)
            summed[j, m] = (own + summed[j, m].astype(F32)).astype(BF16)
        sent(sib, j, summed.at[j])
        go(first, j, summed.at[j, far, 0:64], z_first.at[j, 0], up)
        go(first, j, summed.at[j, far, 64:128], z_first.at[j, 1], down)

    def add_far(j):
        got(first, j, z_first.at[j])
        summed[j, above, 0:64] = (
            summed[j, above, 0:64].astype(F32) + z_first[j, 0].astype(F32)
        ).astype(BF16)
        summed[j, below, 64:128] = (
            summed[j, below, 64:128].astype(F32) + z_first[j, 1].astype(F32)
        ).astype(BF16)
        go(second, j, summed.at[j, above], z_second.at[j, 0], up)
        go(second, j, summed.at[j, below], z_second.at[j, 1], down)
        sent(first, j, z_first.at[j])

    def drift(j):
        got(second, j, z_second.at[j])
        rows = pl.ds(pl.multiple_of((j % 8) * 128, 128), 128)
        for m in range(2):
            lanes = slice(m * 128, (m + 1) * 128)
            total = (
                summed[j, me.z, :, lanes].astype(F32)
                + z_second[j, 0, :, lanes].astype(F32)
                + z_second[j, 1, :, lanes].astype(F32)
            )
            projected = jnp.where((j // 4) % 2 == 1, pltpu.roll(total, 64, 1), total)
            low, high = natural(j, m)
            gate = jnp.where(lower[0:1], mod[2, :, low], mod[2, :, high])
            branch = gate * projected
            acts[0:TOK, low] = jnp.where(lower, branch, acts[0:TOK, low].astype(F32)).astype(BF16)
            acts[0:TOK, high] = jnp.where(lower, acts[0:TOK, high].astype(F32), branch).astype(BF16)
            current = jnp.where(lower, states[:, low], states[:, high])
            anchor = jnp.where(me.step == 0, current, 0.0)
            raw[rows, pl.ds(pl.multiple_of((j // 8) * 256 + m * 128, 128), 128)] = (
                width * (current + branch) + anchor
            )
        pair_out[j] = raw[kept(j, 1 - me.x_lo)].astype(BF16)
        go(pair, j, pair_out.at[j], pair_in.at[j], partner)

        @pl.when(j >= NJ - 4)
        def _():
            update_out(j % 4).start()

        sent(second, j, z_second.at[j])

    def add_pair(j):
        got(pair, j, pair_in.at[j])
        chain_out[j] = (raw[kept(j, me.x_lo)] + pair_in[j].astype(F32)).astype(BF16)
        for d in (1, 2, 3):

            @pl.when(me.y + d < 4)
            def _(d=d):
                go(chain, j, chain_out.at[j], chain_in.at[j, d - 1], later[d - 1])

        sent(pair, j, pair_in.at[j])

    def add_earlier(j):
        for d in (1, 2, 3):

            @pl.when(me.y == d)
            def _(d=d):
                got(chain, j, chain_in.at[j, 0:d])

        earlier = jnp.zeros((64, CW), F32)
        for d in (1, 2, 3):
            earlier = earlier + jnp.where(me.y >= d, chain_in[j, d - 1].astype(F32), 0.0)
        mine = kept(j, me.x_lo)
        own = raw[mine]
        back_out[j] = (earlier + jnp.where(on_low, own, 0.0)).astype(BF16)
        go(back, j, back_out.at[j], back_in.at[j], partner)
        raw[mine] = own + (earlier + jnp.where(on_low, 0.0, pair_in[j].astype(F32)))
        for d in (1, 2, 3):

            @pl.when(me.y + d == 3)
            def _(d=d):
                sent(chain, j, chain_in.at[j, 0:d])

    def add_back(j):
        got(back, j, back_in.at[j])
        other = kept(j, 1 - me.x_lo)
        raw[other] = raw[other] + back_in[j].astype(F32)
        rows = pl.ds(pl.multiple_of((j % 8) * 128, 128), 128)
        for m in range(2):
            low, high = natural(j, m)
            total = raw[rows, pl.ds(pl.multiple_of((j // 8) * 256 + m * 128, 128), 128)]
            states[:, low] = jnp.where(lower, total, states[:, low])
            states[:, high] = jnp.where(lower, states[:, high], total)

        @pl.when(j >= NJ - 4)
        def _():
            next_out(j % 4).start()

        sent(back, j, back_in.at[j])

    with jax.named_scope("reduce"):
        stages = (project, add_sibling, add_far, drift, add_pair, add_earlier, add_back)

        @pl.loop(0, NJ + LAGS[-1])
        def _(i):
            @pl.when(i == 4)
            def _():
                o_b.finish()

            @pl.when(i == 3)
            def _():
                o_c.start4()

            @pl.when(i == 8)
            def _():
                o_c.finish()

            for lag, stage in zip(LAGS, stages):
                j = i - lag

                @pl.when((j >= 0) & (j < NJ))
                def _(stage=stage, j=j):
                    stage(j)

    with jax.named_scope("drain"):
        for g in (o_a, o_b, o_c):
            g.drain()
    with jax.named_scope("results"):
        for n in range(4):
            update_out(n).wait()
            next_out(n).wait()


def body(states, timesteps, lengths, modulation, w_query, w_key, w_value, w_out, q_gain, k_gain):
    n_send = 8 * 4 + 6 + 1 + 6 * FLIGHT
    n_recv = 8 * 6 + 6 + 1 + 5 * AHEAD + NJ
    vmem = pl.BlockSpec(memory_space=pltpu.VMEM)
    smem = pl.BlockSpec(memory_space=pltpu.SMEM)
    anywhere = pl.BlockSpec(memory_space=pl.ANY)
    nxt, update = pl.pallas_call(
        kernel,
        out_shape=(
            jax.ShapeDtypeStruct((TOK, 5120), F32),
            jax.ShapeDtypeStruct((TOK, 5120), BF16),
        ),
        in_specs=[smem, smem, vmem, vmem] + [anywhere] * 6,
        out_specs=(anywhere, anywhere),
        scratch_shapes=[
            pltpu.VMEM((TOK, 5120), F32),
            pltpu.VMEM((3, 1, 5120), F32),
            pltpu.VMEM((1024, 5120), BF16),
            pltpu.VMEM((4, 4, 2, 160, 256), BF16),
            pltpu.VMEM((4, 4, 2, 160, 256), BF16),
            pltpu.VMEM((4, 4, 2, 160, 256), BF16),
            pltpu.VMEM((4, 4, 2, 160, 256), BF16),
            pltpu.VMEM((4, 4, 2, 160, 128), BF16),
            pltpu.VMEM((PIECES, 4, 4, 2, 32, LOCAL), BF16),
            pltpu.VMEM((1024, 2 * LOCAL), F32),
            pltpu.VMEM((1024, 2 * LOCAL), BF16),
            pltpu.VMEM((1024, LOCAL), BF16),
            pltpu.VMEM((3, 1024, 1024), BF16),
            pltpu.VMEM((1024, LOCAL), BF16),
            pltpu.VMEM((8, 16, 128), F32),
            pltpu.VMEM((SLOTS, 4, 2, TOK, CW), BF16),
            pltpu.VMEM((NJ, 4, TOK, CW), BF16),
            pltpu.VMEM((NJ, 2, 64, CW), BF16),
            pltpu.VMEM((NJ, 2, TOK, CW), BF16),
            pltpu.VMEM((NJ, 64, CW), BF16),
            pltpu.VMEM((NJ, 64, CW), BF16),
            pltpu.VMEM((NJ, 64, CW), BF16),
            pltpu.VMEM((NJ, 3, 64, CW), BF16),
            pltpu.VMEM((NJ, 64, CW), BF16),
            pltpu.VMEM((NJ, 64, CW), BF16),
            pltpu.SemaphoreType.DMA((n_send,)),
            pltpu.SemaphoreType.DMA((n_recv,)),
            pltpu.SemaphoreType.DMA((9,)),
        ],
        compiler_params=pltpu.CompilerParams(
            collective_id=0,
            has_side_effects=True,
            vmem_limit_bytes=63 * 1024 * 1024,
        ),
    )(
        lengths,
        timesteps,
        q_gain,
        k_gain,
        states,
        modulation.transpose(1, 0, 2),
        w_query.reshape(2, 160, LOCAL),
        w_key.reshape(2, 160, LOCAL),
        w_value.reshape(2, 160, LOCAL),
        w_out.T.reshape(PIECES, 2, 32, LOCAL),
    )
    return (nxt[None, None], update[None, None])


def solution(mesh):
    in_specs = (
        P("step", "fsdp", "head", None),
        P("step", None),
        P("fsdp"),
        P("step", None, None),
        P(("step", "fsdp"), "head"),
        P(("step", "fsdp"), "head"),
        P(("step", "fsdp"), "head"),
        P("head", ("step", "fsdp")),
        P("head"),
        P("head"),
    )
    out_specs = (P("step", "fsdp", "head", None), P("step", "fsdp", "head", None))
    return jax.shard_map(body, mesh=mesh, in_specs=in_specs, out_specs=out_specs, check_vma=False)
```

time: 162 us -> 154 us (0.951)
  Pallas kernels: 156 us -> 148 us
    pallas_call x1, Pallas kernels: 156 us -> 148 us  [body(): pl.pallas_call(kernel, out_shape=(jax.ShapeDtypeStruct((TOK, 5120), F32),...]
where the time goes in v3:
time: 154 us
  Pallas kernels  148 us (96%)
  local copies, waits for them, and re-layouts  4.65 us (3%)
    pallas_call x1, Pallas kernels, body(): pl.pallas_call(kernel, out_shape=(jax.ShapeDtypeStruct((TOK, 5120), F32),...  148 us
    unnamed x4, local copies, waits for them, and re-layouts  4.65 us

profile of v3, /device:TPU:24, one launch (start us, length us, event | category | flops | bytes accessed | tf_op | source)
XLA Modules:
  0.0 154.3 jit_solution(5790624204013334480)
XLA Ops:
  1.3 148.4 %shard_map.113 = (f32[128,5120]{1,0:T(8,128)}, bf16[128,5120]{1,0:T(8,128)(2,1)}) custom-call(s32[1]{0:T(128)S(6)} %copy.14.length_ref, s32[1,2]{1,0:T(1,128)} %time_ref.1, f32[384]{0:T(512)} %q_gain_ref.1, f32[384]{0:T(512)} %k_gain_ref.1, f32[1,1,128,5120]{3,2,1,0:T(8,128)} %states_hbm.1, f32[3,1,5120]{2,1,0:T(1,128)} %bitcast.15, ...), custom_call_target="tpu_custom_call" | custom-call | tf_op jit(solution)/shard_map/pallas_call | solution.py:709
  149.7 0.0 copy-start
  149.7 3.6 %copy.15 = f32[1,1,128,5120]{3,2,1,0:T(8,128)} copy(f32[1,1,128,5120]{3,2,1,0:T(8,128)} %bitcast.9) | data formatting | bytes 5242880
  153.3 0.0 copy-done
  153.3 1.1 copy.16
Async XLA Ops:
  149.7 3.6 %copy-start = (bf16[128,5120]{1,0:T(8,128)(2,1)S(1)}, bf16[128,5120]{1,0:T(8,128)(2,1)}, u32[]{:S(2)}) copy-start(bf16[128,5120]{1,0:T(8,128)(2,1)} %get-tuple-element.5) | copy-start | bytes 3932164

commit v4 on v3

--- a/solution.py
+++ b/solution.py
@@ -218,8 +218,8 @@
     wk_hbm,
     wv_hbm,
     wo_hbm,
-    next_hbm,
-    update_hbm,
+    next_ref,
+    update_ref,
     states,
     mod,
     acts,
@@ -309,6 +309,9 @@
             spread = jnp.mean(centred * centred, axis=-1, keepdims=True)
             out = centred * lax.rsqrt(spread + 1e-06) * scale + shift
             acts[pl.ds(pl.multiple_of(me.head * TOK + r * 32, 32), 32), :] = out.astype(BF16)
+
+        for h in range(3):
+            value[h, :, HD : 2 * HD] = jnp.ones((1024, HD), BF16)
 
     with jax.named_scope("barrier"):
         local[2].wait()
@@ -365,20 +368,20 @@
         o_a.start1()
     with jax.named_scope("tokens4"):
         tokens.start4()
+    with jax.named_scope("far_wait"):
+        tokens.far_chip()
+    with jax.named_scope("far_ab"):
+        raw_product(2, w_a, 0)
+        raw_product(2, w_b, 1)
     with jax.named_scope("c5"):
         g_c.finish()
-    with jax.named_scope("near_c"):
-
-        @pl.loop(0, 3)
+        g_e.start3()
+    with jax.named_scope("all_c"):
+
+        @pl.loop(0, 4)
         def _(i):
-            raw_product(i + 3, w_c, 2)
-
-    with jax.named_scope("far_wait"):
-        tokens.far_chip()
-    with jax.named_scope("far"):
-        raw_product(2, w_a, 0)
-        raw_product(2, w_b, 1)
-        raw_product(2, w_c, 2)
+            raw_product(i, w_c, 2)
+
     with jax.named_scope("squares"):
 
         @pl.loop(0, 8)
@@ -399,29 +402,30 @@
 
     def softmax(h, m):
         rows = pl.ds(pl.multiple_of(m * 256, 256), 256)
-        valid = lax.broadcasted_iota(jnp.int32, (256, 1024), 1) < length
+        valid = lax.broadcasted_iota(jnp.int32, (256, 512), 1) < length - 512
         q = qk[rows, h * HD : (h + 1) * HD]
         k = qk[:, LOCAL + h * HD : LOCAL + (h + 1) * HD]
         s = lax.dot_general(q, k, (((1,), (1,)), ((), ())), preferred_element_type=F32)
-        s = jnp.where(valid, s * (math.log2(math.e) / math.sqrt(HD)), -jnp.inf)
-        e = jnp.exp2(s - jnp.max(s, axis=-1, keepdims=True))
-        probs[h, rows, :] = (e * (1.0 / jnp.sum(e, axis=-1, keepdims=True))).astype(BF16)
+        s = s * (math.log2(math.e) / math.sqrt(HD))
+        s = jnp.concatenate([s[:, 0:512], jnp.where(valid, s[:, 512:1024], -jnp.inf)], axis=1)
+        probs[h, rows, :] = jnp.exp2(s - jnp.max(s, axis=-1, keepdims=True)).astype(BF16)
 
     def attend(h, m):
         rows = pl.ds(pl.multiple_of(m * 256, 256), 256)
-        o = jnp.dot(probs[h, rows, :], value[:, h * HD : (h + 1) * HD], preferred_element_type=F32)
-        attended[rows, h * HD : (h + 1) * HD] = o.astype(BF16)
-
-    def value_product(w, cols, m):
+        o = jnp.dot(probs[h, rows, :], value[h], preferred_element_type=F32)
+        attended[rows, h * HD : (h + 1) * HD] = (o[:, 0:HD] / o[:, HD : 2 * HD]).astype(BF16)
+
+    def value_product(w, heads, m):
         rows = pl.ds(pl.multiple_of(m * 256, 256), 256)
-        value[rows, cols] = product(rows, w).astype(BF16)
+        v = product(rows, w).astype(BF16)
+        for n, h in enumerate(heads):
+            value[h, rows, 0:HD] = v[:, n * HD : (n + 1) * HD]
 
     with jax.named_scope("d4"):
         g_d.start4()
         o_a.start2()
-        g_e.start3()
         o_b.start1()
-        o_c.start1()
+        g_e.start4()
     with jax.named_scope("squares_wait"):
         link.got(r_squares, squares.at[0:7])
         link.sent(s_squares, squares.at[0:7])
@@ -448,56 +452,39 @@
 
     with jax.named_scope("o_a3"):
         o_a.start3()
-    with jax.named_scope("softmax1"):
+        o_b.start2()
+        o_c.start1()
+    with jax.named_scope("d5"):
+        g_d.finish()
+    with jax.named_scope("softmax1_value_d"):
 
         @pl.loop(0, 4)
         def _(m):
             softmax(1, m)
-
-    with jax.named_scope("d5"):
-        g_d.finish()
-    with jax.named_scope("e4"):
-        g_e.start4()
-        o_b.start2()
-        o_c.start2()
-    with jax.named_scope("value_d"):
-
-        @pl.loop(0, 4)
-        def _(m):
-            value_product(w_d, slice(0, 256), m)
+            value_product(w_d, (0, 1), m)
 
     with jax.named_scope("o_b3"):
         o_a.start4()
         o_b.start3()
-    with jax.named_scope("softmax2"):
+    with jax.named_scope("e5"):
+        g_e.finish()
+        o_c.start2()
+    with jax.named_scope("softmax2_value_e"):
 
         @pl.loop(0, 4)
         def _(m):
             softmax(2, m)
-
-    with jax.named_scope("attend01"):
+            value_product(w_e, (2,), m)
+
+    with jax.named_scope("o_b4"):
+        o_b.start4()
+        o_c.start3()
+    with jax.named_scope("attend"):
 
         @pl.loop(0, 4)
         def _(m):
-            attend(0, m)
-            attend(1, m)
-
-    with jax.named_scope("e5"):
-        g_e.finish()
-        o_c.start3()
-    with jax.named_scope("value_e"):
-
-        @pl.loop(0, 4)
-        def _(m):
-            value_product(w_e, slice(256, 384), m)
-
-    with jax.named_scope("o_b4"):
-        o_b.start4()
-    with jax.named_scope("attend2"):
-
-        @pl.loop(0, 4)
-        def _(m):
-            attend(2, m)
+            for h in range(3):
+                attend(h, m)
 
     with jax.named_scope("o_a5"):
         o_a.finish()
@@ -528,17 +515,6 @@
 
     def sent(kind, j, size):
         link.sent(send_of(kind, j), size)
-
-    def quarter(n):
-        return pl.ds(pl.multiple_of(n * 1280, 128), 1280)
-
-    def next_out(n):
-        return pltpu.make_async_copy(states.at[:, quarter(n)], next_hbm.at[:, quarter(n)], local_sem.at[n])
-
-    def update_out(n):
-        return pltpu.make_async_copy(
-            acts.at[0:TOK, quarter(n)], update_hbm.at[:, quarter(n)], local_sem.at[4 + n]
-        )
 
     def natural(j, m):
         piece, tile = j // 4, (j % 4) * 2 + m
@@ -602,8 +578,8 @@
             low, high = natural(j, m)
             gate = jnp.where(lower[0:1], mod[2, :, low], mod[2, :, high])
             branch = gate * projected
-            acts[0:TOK, low] = jnp.where(lower, branch, acts[0:TOK, low].astype(F32)).astype(BF16)
-            acts[0:TOK, high] = jnp.where(lower, acts[0:TOK, high].astype(F32), branch).astype(BF16)
+            update_ref[:, low] = jnp.where(lower, branch, update_ref[:, low].astype(F32)).astype(BF16)
+            update_ref[:, high] = jnp.where(lower, update_ref[:, high].astype(F32), branch).astype(BF16)
             current = jnp.where(lower, states[:, low], states[:, high])
             anchor = jnp.where(me.step == 0, current, 0.0)
             raw[rows, pl.ds(pl.multiple_of((j // 8) * 256 + m * 128, 128), 128)] = (
@@ -611,11 +587,6 @@
             )
         pair_out[j] = raw[kept(j, 1 - me.x_lo)].astype(BF16)
         go(pair, j, pair_out.at[j], pair_in.at[j], partner)
-
-        @pl.when(j >= NJ - 4)
-        def _():
-            update_out(j % 4).start()
-
         sent(second, j, z_second.at[j])
 
     def add_pair(j):
@@ -658,13 +629,8 @@
         for m in range(2):
             low, high = natural(j, m)
             total = raw[rows, pl.ds(pl.multiple_of((j // 8) * 256 + m * 128, 128), 128)]
-            states[:, low] = jnp.where(lower, total, states[:, low])
-            states[:, high] = jnp.where(lower, states[:, high], total)
-
-        @pl.when(j >= NJ - 4)
-        def _():
-            next_out(j % 4).start()
-
+            next_ref[:, low] = jnp.where(lower, total, next_ref[:, low])
+            next_ref[:, high] = jnp.where(lower, next_ref[:, high], total)
         sent(back, j, back_in.at[j])
 
     with jax.named_scope("reduce"):
@@ -676,7 +642,7 @@
             def _():
                 o_b.finish()
 
-            @pl.when(i == 3)
+            @pl.when(i == 6)
             def _():
                 o_c.start4()
 
@@ -694,10 +660,6 @@
     with jax.named_scope("drain"):
         for g in (o_a, o_b, o_c):
             g.drain()
-    with jax.named_scope("results"):
-        for n in range(4):
-            update_out(n).wait()
-            next_out(n).wait()
 
 
 def body(states, timesteps, lengths, modulation, w_query, w_key, w_value, w_out, q_gain, k_gain):
@@ -709,11 +671,11 @@
     nxt, update = pl.pallas_call(
         kernel,
         out_shape=(
-            jax.ShapeDtypeStruct((TOK, 5120), F32),
-            jax.ShapeDtypeStruct((TOK, 5120), BF16),
+            pltpu.VMEM((TOK, 5120), F32),
+            pltpu.VMEM((TOK, 5120), BF16),
         ),
         in_specs=[smem, smem, vmem, vmem] + [anywhere] * 6,
-        out_specs=(anywhere, anywhere),
+        out_specs=(vmem, vmem),
         scratch_shapes=[
             pltpu.VMEM((TOK, 5120), F32),
             pltpu.VMEM((3, 1, 5120), F32),
@@ -726,7 +688,7 @@
             pltpu.VMEM((PIECES, 4, 4, 2, 32, LOCAL), BF16),
             pltpu.VMEM((1024, 2 * LOCAL), F32),
             pltpu.VMEM((1024, 2 * LOCAL), BF16),
-            pltpu.VMEM((1024, LOCAL), BF16),
+            pltpu.VMEM((3, 1024, 2 * HD), BF16),
             pltpu.VMEM((3, 1024, 1024), BF16),
             pltpu.VMEM((1024, LOCAL), BF16),
             pltpu.VMEM((8, 16, 128), F32),
@@ -747,7 +709,7 @@
         compiler_params=pltpu.CompilerParams(
             collective_id=0,
             has_side_effects=True,
-            vmem_limit_bytes=63 * 1024 * 1024,
+            vmem_limit_bytes=57 * 1024 * 1024,
         ),
     )(
         lengths,

time: 154 us -> 150 us (0.974)
  local copies, waits for them, and re-layouts: 4.65 us -> 2.55 us
  Pallas kernels: 148 us -> 146 us
    pallas_call x1, Pallas kernels: 148 us -> 146 us  [body(): pl.pallas_call(kernel, out_shape=(pltpu.VMEM((TOK, 5120), F32), pltpu.VME...]
    unnamed x4 -> x2, local copies, waits for them, and re-layouts: 4.65 us -> 2.55 us
where the time goes in v4:
time: 150 us
  Pallas kernels  146 us (97%)
  local copies, waits for them, and re-layouts  2.55 us (2%)
    pallas_call x1, Pallas kernels, body(): pl.pallas_call(kernel, out_shape=(pltpu.VMEM((TOK, 5120), F32), pltpu.VME...  146 us

profile of v4, /device:TPU:24, one launch (start us, length us, event | category | flops | bytes accessed | tf_op | source)
XLA Modules:
  0.0 149.7 jit_solution(4596090721708432564)
XLA Ops:
  1.3 145.9 %shard_map.113 = (f32[128,5120]{1,0:T(8,128)S(1)}, bf16[128,5120]{1,0:T(8,128)(2,1)S(1)}) custom-call(s32[1]{0:T(128)S(6)} %copy.16.length_ref, s32[1,2]{1,0:T(1,128)} %time_ref.1, f32[384]{0:T(512)} %q_gain_ref.1, f32[384]{0:T(512)} %k_gain_ref.1, f32[1,1,128,5120]{3,2,1,0:T(8,128)} %states_hbm.1, f32[3,1,5120]{2,1,0:T(1,128)} %bitcast.15, ...), custom_call_target="tpu_custom_call" | custom-call | tf_op jit(solution)/shard_map/pallas_call | solution.py:671
  147.1 1.5 copy.14
  148.6 1.1 copy.15

commit v5 on v4

--- a/solution.py
+++ b/solution.py
@@ -16,8 +16,8 @@
 PIECES = 5
 NJ = 20
 CW = 256
-LAGS = (0, 1, 3, 5, 7, 9, 11)
-SLOTS = 2
+LAGS = (0, 2, 5, 8, 10, 12, 14)
+SLOTS = 3
 FLIGHT = 4
 AHEAD = 8
 

time: 150 us -> 149 us (level)
  no operation moved by 1% of the time
where the time goes in v5:
time: 149 us
  Pallas kernels  145 us (97%)
  local copies, waits for them, and re-layouts  2.55 us (2%)
    pallas_call x1, Pallas kernels, body(): pl.pallas_call(kernel, out_shape=(pltpu.VMEM((TOK, 5120), F32), pltpu.VME...  145 us

profile of v5, /device:TPU:24, one launch (start us, length us, event | category | flops | bytes accessed | tf_op | source)
XLA Modules:
  0.0 148.6 jit_solution(5470727724188844120)
XLA Ops:
  1.3 144.7 %shard_map.113 = (f32[128,5120]{1,0:T(8,128)S(1)}, bf16[128,5120]{1,0:T(8,128)(2,1)S(1)}) custom-call(s32[1]{0:T(128)S(6)} %copy.16.length_ref, s32[1,2]{1,0:T(1,128)} %time_ref.1, f32[384]{0:T(512)} %q_gain_ref.1, f32[384]{0:T(512)} %k_gain_ref.1, f32[1,1,128,5120]{3,2,1,0:T(8,128)} %states_hbm.1, f32[3,1,5120]{2,1,0:T(1,128)} %bitcast.15, ...), custom_call_target="tpu_custom_call" | custom-call | tf_op jit(solution)/shard_map/pallas_call | solution.py:671
  146.0 1.5 %copy.14 = f32[1,1,128,5120]{3,2,1,0:T(8,128)} copy(f32[1,1,128,5120]{3,2,1,0:T(8,128)S(1)} %bitcast.9) | data formatting | bytes 5242880
  147.5 1.1 copy.15

commit v6 on v5

--- a/solution.py
+++ b/solution.py
@@ -80,7 +80,7 @@
         below, above, far_y = me.row(-1), me.row(1), me.row(2)
         east, west, north, south = me.at(dx=1), me.at(dx=-1), me.at(dy=1), me.at(dy=-1)
         self.link, self.view = link, view
-        self.s, self.r = link.take(4, 6)
+        self.s, self.r = link.take(4, 4)
         self.sends = (
             ((y, c, 0, whole), east),
             ((y, c, 0, whole), west),
@@ -109,8 +109,7 @@
         for slot in range(first, last):
             args, to = self.sends[slot]
             part = self.view(*args)
-            recv = (0, 0, 1, 1, 2, 2, 2, 2, 3, 3, 4, 4, 5, 5, 5, 5)[slot]
-            self.link.copy(part, part, self.s + slot // 4, self.r + recv, to).start()
+            self.link.copy(part, part, self.s + slot // 4, self.r + slot // 4, to).start()
 
     def got(self, n, size):
         self.link.got(self.r + n, size)
@@ -119,23 +118,19 @@
         self.start(0, 4)
 
     def start2(self):
-        self.got(0, self.pair)
-        self.start(4, 6)
+        self.got(0, self.row)
+        self.start(4, 8)
+
+    def start3(self):
         self.got(1, self.pair)
-        self.start(6, 8)
-
-    def start3(self):
-        self.got(2, self.pair)
         self.start(8, 12)
 
     def start4(self):
+        self.got(2, self.half)
+        self.start(12, 16)
+
+    def finish(self):
         self.got(3, self.rows)
-        self.start(12, 14)
-        self.got(4, self.rows)
-        self.start(14, 16)
-
-    def finish(self):
-        self.got(5, self.rows)
 
     def drain(self):
         for phase, size in enumerate((self.row, self.pair, self.half, self.rows)):
@@ -664,7 +659,7 @@
 
 def body(states, timesteps, lengths, modulation, w_query, w_key, w_value, w_out, q_gain, k_gain):
     n_send = 8 * 4 + 6 + 1 + 6 * FLIGHT
-    n_recv = 8 * 6 + 6 + 1 + 5 * AHEAD + NJ
+    n_recv = 8 * 4 + 6 + 1 + 5 * AHEAD + NJ
     vmem = pl.BlockSpec(memory_space=pltpu.VMEM)
     smem = pl.BlockSpec(memory_space=pltpu.SMEM)
     anywhere = pl.BlockSpec(memory_space=pl.ANY)

time: 149 us -> 149 us (level)
  no operation moved by 1% of the time
where the time goes in v6:
time: 149 us; the launch traced here: 148 us
  Pallas kernels  145 us (97%)
  local copies, waits for them, and re-layouts  2.55 us (2%)
    pallas_call x1, Pallas kernels, body(): pl.pallas_call(kernel, out_shape=(pltpu.VMEM((TOK, 5120), F32), pltpu.VME...  145 us

profile of v6, /device:TPU:24, one launch (start us, length us, event | category | flops | bytes accessed | tf_op | source)
XLA Modules:
  0.0 148.4 jit_solution(14867303189019552629)
XLA Ops:
  1.3 144.6 %shard_map.113 = (f32[128,5120]{1,0:T(8,128)S(1)}, bf16[128,5120]{1,0:T(8,128)(2,1)S(1)}) custom-call(s32[1]{0:T(128)S(6)} %copy.16.length_ref, s32[1,2]{1,0:T(1,128)} %time_ref.1, f32[384]{0:T(512)} %q_gain_ref.1, f32[384]{0:T(512)} %k_gain_ref.1, f32[1,1,128,5120]{3,2,1,0:T(8,128)} %states_hbm.1, f32[3,1,5120]{2,1,0:T(1,128)} %bitcast.15, ...), custom_call_target="tpu_custom_call" | custom-call | tf_op jit(solution)/shard_map/pallas_call | solution.py:666
  145.8 1.5 %copy.14 = f32[1,1,128,5120]{3,2,1,0:T(8,128)} copy(f32[1,1,128,5120]{3,2,1,0:T(8,128)S(1)} %bitcast.9) | data formatting | bytes 5242880
  147.3 1.1 copy.15
